TPU v7x, 32 devices: a whole 2x2x4 slice. The times are simulated.
32 devices in a mesh: dom: 2 (over y), feat: 4 (over z), dp: 4 (over x, core).
Axes of the slice: x: 2, y: 2, z: 4, core: 2. Of those that a mesh axis runs over, the one named last changes fastest.
Arguments:
- layer_in: bfloat16 [32768, 2048], P(('dom', 'dp', 'feat')), parts along dimension 0, may hold values from -6 to 6
- grad_out: bfloat16 [32768, 2048], P(('dom', 'dp', 'feat')), parts along dimension 0, may hold values from -6 to 6
- in_proj: bfloat16 [2048, 256], replicated, may hold values from -0.125 to 0.125
- out_proj: bfloat16 [2048, 256], replicated, may hold values from -0.125 to 0.125
- queries: bfloat16 [2048, 65536], P(('dom', 'dp'), 'feat'), parts along dimension 0, may hold values from -0.00390625 to 0.00390625
- seq_ids: int32 [32, 1024], P(('dom', 'dp', 'feat')), parts along dimension 0, may hold values from 0 to 15, never falling along the last dimension, each value on 1 to 128 neighbouring positions
- valid_counts: int32 [512], P(('dom', 'dp', 'feat')), parts along dimension 0, may hold values from 16 to 128
- owner_order: int32 [2048], P(('dom', 'dp')), parts along dimension 0, may hold values from 0 to 1023, as said below
Outputs:
- scores: float32 [2048, 256], P(('dom', 'dp', 'feat')), parts along dimension 0
There are 2 independent parts, one for each index of `dom`. A program takes and returns all parts, laid end to end along the dimension named above; an argument that names none is the same for every part. Nothing has to cross between parts.
Inputs may be any that keep to these rules, and one draw needn't show every extreme that they name: `seq_ids`: each row numbers the 16 sequences of one block in order, never falling; every number appears. `owner_order`: within each aligned block of 256 rows, a permutation of that block's row numbers.
All inputs are finite; a program needn't handle non-finite values.
Results may differ from a plain program's by a relative error of at most 0.005.
Values may be sent and summed in bfloat16 or wider, within the bound.
No kernel may reach another device: no remote copies, remote signals or barrier semaphores. Data moves between devices by JAX's collectives and lax.ppermute only.
A program may use at most 64 MiB of HBM per device.

v0:
```python
import jax
import jax.numpy as jnp
from jax import lax
from jax.sharding import PartitionSpec as P

WIN = 128


def local(layer_in, grad_out, in_proj, out_proj, queries, seq_ids, valid_counts, owner_order):
    in_low = jnp.dot(layer_in, in_proj, preferred_element_type=jnp.float32).astype(jnp.bfloat16)
    out_low = jnp.dot(grad_out, out_proj, preferred_element_type=jnp.float32).astype(jnp.bfloat16)
    proj_width = in_proj.shape[1]
    seq_count = valid_counts.shape[0]
    labels = seq_ids[0]
    member = (labels[:, None] == jnp.arange(seq_count, dtype=jnp.int32)[None, :]).astype(jnp.int32)
    seg_len = jnp.sum(member, axis=0)
    starts = jnp.cumsum(seg_len) - seg_len
    keep_len = jnp.minimum(seg_len, valid_counts)
    padding = jnp.zeros((WIN, proj_width), jnp.bfloat16)
    in_pad = jnp.concatenate([in_low, padding], axis=0)
    out_pad = jnp.concatenate([out_low, padding], axis=0)

    def windows(first_row):
        return (
            lax.dynamic_slice_in_dim(in_pad, first_row, WIN, 0),
            lax.dynamic_slice_in_dim(out_pad, first_row, WIN, 0),
        )

    in_win, out_win = jax.vmap(windows)(starts)
    usable = jnp.arange(WIN, dtype=jnp.int32)[None, :] < keep_len[:, None]
    in_win = jnp.where(usable[:, :, None], in_win, jnp.zeros((), jnp.bfloat16))
    seq_grads = jnp.einsum("swi,swj->sij", in_win, out_win, preferred_element_type=jnp.float32)
    seq_grads = seq_grads.astype(jnp.bfloat16).reshape(seq_count, proj_width * proj_width)
    train_rows = lax.all_to_all(seq_grads, "feat", split_axis=1, concat_axis=0, tiled=True)
    query_rows = queries.shape[0]
    ordered = jnp.take(queries, owner_order % query_rows, axis=0)
    scored = lax.dot_general(
        ordered,
        lax.all_gather(train_rows, "dp", axis=0, tiled=True),
        (((1,), (1,)), ((), ())),
        preferred_element_type=jnp.float32,
    )
    result = lax.psum_scatter(scored, "feat", scatter_dimension=0, tiled=True)
    return result


def solution(mesh):
    in_specs = (
        P(("dom", "dp", "feat"), None),
        P(("dom", "dp", "feat"), None),
        P(),
        P(),
        P(("dom", "dp"), "feat"),
        P(("dom", "dp", "feat"), None),
        P(("dom", "dp", "feat")),
        P(("dom", "dp")),
    )
    out_specs = P(("dom", "dp", "feat"), None)
    return jax.shard_map(local, mesh=mesh, in_specs=in_specs, out_specs=out_specs, check_vma=False)
```

profile of v0, /device:TPU:0, one launch (start us, length us, event | category | flops | bytes accessed | tf_op | source)
XLA Modules:
  0.0 213.8 jit_solution(496399708918642620)
XLA Ops:
  6.5 0.9 convert_reduce_fusion
  7.4 0.7 min.3
  8.4 3.4 %convolution_convert_fusion.1 = bf16[1024,256]{1,0:T(8,128)(2,1)S(1)} fusion(bf16[1024,2048]{1,0:T(8,128)(2,1)} %param.9, bf16[2048,256]{1,0:T(8,128)(2,1)S(1)} %copy-done), kind=kOutput, calls=%fused_computation.10 | convolution fusion | flops 1074003968 | bytes 5767168 | tf_op jit(solution)/shard_map/dot_general | solution.py:11
  12.0 20.2 %while.3 = (s32[]{:T(128)}, bf16[1152,256]{1,0:T(8,128)(2,1)S(1)}, s32[16,2]{0,1:T(2,128)S(1)}, bf16[16,128,256]{2,1,0:T(8,128)(2,1)S(1)}, s32[]{:T(128)}) while((s32[]{:T(128)}, bf16[1152,256]{1,0:T(8,128)(2,1)S(1)}, s32[16,2]{0,1:T(2,128)S(1)}, bf16[16,128,256]{2,1,0:T(8,128)(2,1)S(1)}, s32[]{:T(128)}) %tuple.34), condition=%wide.while_cond.1, body=%wide.while_body.1.sunk | while | flops 2 | bytes 131177 | solution.py:26
  12.6 0.6 bitcast_dynamic-update-slice_fusion.5
  13.9 0.6 bitcast_dynamic-update-slice_fusion.5
  15.1 0.6 bitcast_dynamic-update-slice_fusion.5
  16.4 0.6 bitcast_dynamic-update-slice_fusion.5
  17.1 0.5 slice.27
  17.6 0.6 bitcast_dynamic-update-slice_fusion.5
  18.9 0.6 bitcast_dynamic-update-slice_fusion.5
  20.2 0.6 bitcast_dynamic-update-slice_fusion.5
  21.4 0.6 bitcast_dynamic-update-slice_fusion.5
  22.7 0.6 bitcast_dynamic-update-slice_fusion.5
  24.0 0.6 bitcast_dynamic-update-slice_fusion.5
  25.2 0.6 bitcast_dynamic-update-slice_fusion.5
  26.5 0.6 bitcast_dynamic-update-slice_fusion.5
  27.7 0.6 bitcast_dynamic-update-slice_fusion.5
  29.0 0.6 bitcast_dynamic-update-slice_fusion.5
  30.3 0.6 bitcast_dynamic-update-slice_fusion.5
  31.5 0.6 bitcast_dynamic-update-slice_fusion.5
  32.2 4.1 %convolution_convert_fusion.2 = bf16[1024,256]{1,0:T(8,128)(2,1)S(1)} fusion(bf16[1024,2048]{1,0:T(8,128)(2,1)} %param.8, bf16[2048,256]{1,0:T(8,128)(2,1)} %param.10), kind=kOutput, calls=%fused_computation.11 | convolution fusion | flops 1074003968 | bytes 5767168 | tf_op jit(solution)/shard_map/dot_general | solution.py:10
  36.5 20.5 %while.2 = (s32[]{:T(128)}, bf16[1152,256]{1,0:T(8,128)(2,1)S(1)}, s32[16,2]{0,1:T(2,128)S(1)}, bf16[16,128,256]{2,1,0:T(8,128)(2,1)S(1)}, s32[]{:T(128)}) while((s32[]{:T(128)}, bf16[1152,256]{1,0:T(8,128)(2,1)S(1)}, s32[16,2]{0,1:T(2,128)S(1)}, bf16[16,128,256]{2,1,0:T(8,128)(2,1)S(1)}, s32[]{:T(128)}) %tuple.44), condition=%wide.while_cond, body=%wide.while_body.sunk | while | flops 2 | bytes 131177 | solution.py:25
  37.1 0.7 bitcast_dynamic-update-slice_fusion.4
  38.3 0.7 bitcast_dynamic-update-slice_fusion.4
  39.6 0.7 bitcast_dynamic-update-slice_fusion.4
  40.9 0.7 bitcast_dynamic-update-slice_fusion.4
  42.2 0.7 bitcast_dynamic-update-slice_fusion.4
  43.5 0.7 bitcast_dynamic-update-slice_fusion.4
  44.7 0.7 bitcast_dynamic-update-slice_fusion.4
  46.0 0.7 bitcast_dynamic-update-slice_fusion.4
  47.3 0.7 bitcast_dynamic-update-slice_fusion.4
  48.6 0.7 bitcast_dynamic-update-slice_fusion.4
  49.9 0.7 bitcast_dynamic-update-slice_fusion.4
  51.1 0.7 bitcast_dynamic-update-slice_fusion.4
  52.4 0.7 bitcast_dynamic-update-slice_fusion.4
  53.7 0.7 bitcast_dynamic-update-slice_fusion.4
  55.0 0.7 bitcast_dynamic-update-slice_fusion.4
  56.3 0.7 bitcast_dynamic-update-slice_fusion.4
  57.0 1.0 copy-done.1
  58.0 2.7 %convolution_convert_fusion = bf16[16,256,256]{2,1,0:T(8,128)(2,1)S(1)} fusion(bf16[16,128,256]{2,1,0:T(8,128)(2,1)} %copy-done.2, bf16[16,128,256]{2,1,0:T(8,128)(2,1)} %copy-done.1, pred[16,128]{1,0:T(8,128)(4,1)S(1)} %iota_compare_fusion.1), kind=kOutput, calls=%fused_computation.9 | convolution fusion | flops 270008320 | bytes 4196352 | tf_op jit(solution)/shard_map/swi,swj->sij/dot_general | solution.py:32
  60.6 2.8 %all_to_all.14 = bf16[16,4,16384]{2,1,0:T(4,128)(2,1)} reshape(bf16[16,256,256]{2,1,0:T(8,128)(2,1)S(1)} %convolution_convert_fusion) | data formatting | bytes 4194304 | tf_op jit(solution)/shard_map/all_to_all | solution.py:34
  63.4 2.7 %copy.25 = bf16[16,4,16384]{2,0,1:T(8,128)(2,1)S(1)} copy(bf16[16,4,16384]{2,1,0:T(4,128)(2,1)} %all_to_all.14) | data formatting | bytes 4194304 | tf_op jit(solution)/shard_map/all_to_all | solution.py:34
  66.1 54.4 %all_to_all.19 = bf16[16,4,16384]{2,0,1:T(8,128)(2,1)} all-to-all(bf16[16,4,16384]{2,0,1:T(8,128)(2,1)S(1)} %copy.25), channel_id=1, replica_groups=mesh['dom'=2,'feat'=4,'dp'=4] {'feat'}, dimensions={1} | all-to-all | bytes 4194304 | tf_op jit(solution)/shard_map/all_to_all | solution.py:34
  120.9 21.0 %gather_fusion = bf16[256,16384]{1,0:T(8,128)(2,1)} fusion(bf16[256,16384]{1,0:T(8,128)(2,1)} %param.12, s32[1024]{0:T(1024)S(1)} %pad_clamp_fusion), kind=kCustom, calls=%fused_computation | custom fusion | bytes 16778240 | tf_op jit(solution)/shard_map/jit(_take)/gather | solution.py:36
  141.9 36.4 %all-gather.2.cloned.1.call-done = bf16[256,16384]{1,0:T(8,128)(2,1)} async-done(((bf16[64,16384]{1,0:T(8,128)(2,1)}), bf16[256,16384]{1,0:T(8,128)(2,1)}) %all-gather.2.cloned.1.call-update) | async-done | bytes 8388624 | tf_op jit(solution)/shard_map/all_gather | solution.py:39
  178.3 8.8 %fusion = f32[256,256]{1,0:T(8,128)} fusion(bf16[256,16384]{1,0:T(8,128)(2,1)} %all-gather.2.cloned.1.call-done, bf16[256,16384]{1,0:T(8,128)(2,1)} %gather_fusion, pred[256]{0:T(512)(128)(4,1)S(1)} %get-tuple-element.61), kind=kOutput, calls=%fused_computation.5 | convolution fusion | flops 2151677952 | bytes 17039616 | tf_op jit(solution)/shard_map/dot_general | solution.py:37
  187.1 19.8 %reduce-scatter.2.cloned.1.call-done = f32[64,256]{1,0:T(8,128)} async-done(((f32[256,256]{1,0:T(8,128)}), f32[64,256]{1,0:T(8,128)}) %reduce-scatter.2.cloned.1.call-update) | async-done | bytes 65552 | tf_op jit(solution)/shard_map/reduce_scatter | solution.py:43
  (86 shorter events, 19.3 us)
Async XLA Ops:
  6.5 1.9 copy-start
  6.5 171.7 %all-gather.2.cloned.1.call-start = ((), (), s32[]{:S(2)}) async-start(), calls=%async_computation.2 | async-start | bytes 10485760 | tf_op jit(solution)/shard_map/all_gather | solution.py:39
  32.2 4.1 %copy-start.2 = (bf16[16,128,256]{2,1,0:T(8,128)(2,1)}, bf16[16,128,256]{2,1,0:T(8,128)(2,1)S(1)}, u32[]{:S(2)}) copy-start(bf16[16,128,256]{2,1,0:T(8,128)(2,1)S(1)} %get-tuple-element.20) | copy-start | bytes 3145732
  57.0 1.0 copy-start.1
  60.6 60.2 %copy-start.3 = (s32[256]{0:T(256)S(1)}, s32[256]{0:T(256)}, u32[]{:S(2)}) copy-start(s32[256]{0:T(256)} %param.15) | copy-start | bytes 3076
  120.6 86.3 %reduce-scatter.2.cloned.1.call-start = ((), (), s32[]{:S(2)}) async-start(), calls=%async_computation.3 | async-start | bytes 327680 | tf_op jit(solution)/shard_map/reduce_scatter | solution.py:43
Sparse Core Ops, SparseCore 0:
  120.7 57.4 all-gather.1
  187.2 19.6 reduce-scatter.1
where the time goes:
time: 214 us
  local copies, waits for them, and re-layouts  67.9 us (32%)
  waiting for transfers between devices  56.2 us (26%)
  blocking collectives  54.4 us (25%)
  matrix products  19 us (9%)
  between operations  13.5 us (6%)
    all_to_all x1, blocking collectives, local(): lax.all_to_all(seq_grads, 'feat', split_axis=1, concat_axis=0, tiled=True)  54.4 us
    gather x96, local copies, waits for them, and re-layouts  39.9 us
    all_gather x1, waiting for transfers between devices, local(): lax.all_gather(train_rows, 'dp', axis=0, tiled=True)  36.4 us
    gather x1, local copies, waits for them, and re-layouts, local(): ordered = jnp.take(queries, owner_order % query_rows, axis=0)  21 us
    reduce_scatter x1, waiting for transfers between devices, local(): result = lax.psum_scatter(scored, 'feat', scatter_dimension=0, tiled=True)  19.8 us
    dot_general x1, matrix products, local(): lax.dot_general(ordered, lax.all_gather(train_rows, 'dp', axis=0, tiled=T...  8.84 us
    all_to_all x2, local copies, waits for them, and re-layouts, local(): lax.all_to_all(seq_grads, 'feat', split_axis=1, concat_axis=0, tiled=True)  5.5 us
  transfers between devices with their start and end apart: 2, of which 2 were waited for; matrix products, arithmetic and copies ran while one was open for 10% of the time, Pallas kernels for 0%

commit v1 on v0

v1 whole, which is shorter than its diff:
```python
import functools

import jax
import jax.numpy as jnp
from jax import lax
from jax.experimental import pallas as pl
from jax.experimental.pallas import tpu as pltpu
from jax.sharding import PartitionSpec as P

F32 = jnp.float32
BF16 = jnp.bfloat16
NT = (((1,), (1,)), ((), ()))
MIB = 1 << 20
TOKEN_BLOCK = 256
ROW_BLOCK = 16
TURN_BLOCK = 2048
FREE = pl.CostEstimate(flops=0, bytes_accessed=0, transcendentals=0)
IN_HBM = pl.BlockSpec(memory_space=pltpu.HBM)
IN_VMEM = pl.BlockSpec(memory_space=pltpu.VMEM)
PARAMS = pltpu.CompilerParams(vmem_limit_bytes=16 * MIB)


def hbm(array):
    return pltpu.with_memory_space_constraint(array, pltpu.HBM)


def counted_mask(ids, valid):
    seqs, tokens = valid.shape[1], ids.shape[1]
    eye = lax.broadcasted_iota(jnp.int32, (seqs, seqs), 0) == lax.broadcasted_iota(jnp.int32, (seqs, seqs), 1)
    limit = jnp.sum(jnp.where(eye, jnp.broadcast_to(valid, (seqs, seqs)), 0), axis=1, keepdims=True)
    ids = jnp.broadcast_to(ids, (seqs, tokens))
    seq = lax.broadcasted_iota(jnp.int32, (seqs, tokens), 0)
    start = jnp.sum((ids < seq).astype(jnp.int32), axis=1, keepdims=True)
    position = lax.broadcasted_iota(jnp.int32, (seqs, tokens), 1) - start
    return jnp.where((ids == seq) & (position < limit), 1.0, 0.0).astype(F32)


def grads_kernel(parts, ask, layer, grad, in_proj, out_proj, ids, valid, *rest):
    outs = rest[: len(ask)]
    layer_v, grad_v, in_v, out_v, ids_v, valid_v, in_t, out_low, mask, sems = rest[len(ask):]
    tokens = layer.shape[0]
    block = min(TOKEN_BLOCK, tokens)
    spans = [pl.ds(t, block) for t in range(0, tokens, block)]
    copies = []

    def fetch(source, target):
        copy = pltpu.make_async_copy(source, target, sems.at[len(copies)])
        copy.start()
        copies.append(copy)
        return copy

    out_copy = fetch(out_proj, out_v)
    grad_copies = [fetch(grad.at[spans[0]], grad_v.at[spans[0]])]
    small_copies = [fetch(ids, ids_v), fetch(valid, valid_v)]
    grad_copies += [fetch(grad.at[s], grad_v.at[s]) for s in spans[1:]]
    in_copy = fetch(in_proj, in_v)
    layer_copies = [fetch(layer.at[s], layer_v.at[s]) for s in spans]
    for copy in small_copies:
        copy.wait()
    mask[...] = counted_mask(ids_v[...], valid_v[...])
    out_copy.wait()
    for s, copy in zip(spans, grad_copies):
        copy.wait()
        out_low[s, :] = jnp.dot(grad_v[s, :], out_v[...], preferred_element_type=F32).astype(BF16)
    in_copy.wait()
    for s, copy in zip(spans, layer_copies):
        copy.wait()
        low = jnp.dot(layer_v[s, :], in_v[...], preferred_element_type=F32).astype(BF16)
        in_t[:, s] = low.astype(F32).T
    width = in_t.shape[0]
    seqs = mask.shape[0]
    span = width // parts
    me = lax.axis_index("feat")
    for (k, piece, pieces), out in zip(ask, outs):
        size = span // pieces
        small = min(ROW_BLOCK, size)
        base = pl.multiple_of((me ^ k) * span + piece * size, size)
        for r in range(0, size, small):
            rows = in_t[pl.ds(base + r, small), :]
            left = (rows[:, None, :] * mask[...][None]).astype(BF16).reshape(small * seqs, tokens)
            got = jnp.dot(left, out_low[...], preferred_element_type=F32).astype(BF16)
            out[pl.ds(r, small)] = got.reshape(small, seqs, got.shape[1])


def grads(parts, ask, layer_in, grad_out, in_proj, out_proj, seq_ids, valid_counts):
    tokens, model = layer_in.shape
    width = in_proj.shape[1]
    seqs = valid_counts.shape[0]
    block = min(TOKEN_BLOCK, tokens)
    args = (layer_in, grad_out, in_proj, out_proj, seq_ids, valid_counts.reshape(1, seqs))
    return pl.pallas_call(
        functools.partial(grads_kernel, parts, ask),
        in_specs=[IN_HBM] * 6,
        out_specs=[IN_VMEM] * len(ask),
        out_shape=[pltpu.VMEM((width // parts // part[2], seqs, width), BF16) for part in ask],
        scratch_shapes=[
            pltpu.VMEM((tokens, model), BF16),
            pltpu.VMEM((tokens, model), BF16),
            pltpu.VMEM((model, width), BF16),
            pltpu.VMEM((model, width), BF16),
            pltpu.VMEM((1, tokens), jnp.int32),
            pltpu.VMEM((1, seqs), jnp.int32),
            pltpu.VMEM((width, tokens), F32),
            pltpu.VMEM((tokens, width), BF16),
            pltpu.VMEM((seqs, tokens), F32),
            pltpu.SemaphoreType.DMA((4 + 2 * (tokens // block),)),
        ],
        compiler_params=PARAMS,
        cost_estimate=FREE,
        name="sequence_grads",
    )(*map(hbm, args))


def turn_kernel(source, out, held, sems):
    depth = source.shape[1]
    block = min(TURN_BLOCK, depth)
    copies = []
    for n, start in enumerate(range(0, depth, block)):
        span = pl.ds(start, block)
        copies.append(pltpu.make_async_copy(source.at[:, span], held.at[:, span], sems.at[n]))
        copies[-1].start()
    for n, start in enumerate(range(0, depth, block)):
        copies[n].wait()
        span = pl.ds(start, block)
        out[span, :] = held[:, span].T


def turn(queries):
    rows, depth = queries.shape
    return pl.pallas_call(
        turn_kernel,
        in_specs=[IN_HBM],
        out_specs=IN_VMEM,
        out_shape=pltpu.VMEM((depth, rows), BF16),
        scratch_shapes=[pltpu.VMEM((rows, depth), BF16), pltpu.SemaphoreType.DMA((-(-depth // TURN_BLOCK),))],
        compiler_params=PARAMS,
        cost_estimate=FREE,
        name="turn",
    )(hbm(queries))


def score_kernel(offset, count, first, last, *rest):
    rest = list(rest)
    queries = [rest.pop(0), rest.pop(0)]
    pieces = [rest.pop(0) for _ in range(count)]
    totals = [None, None] if first else [rest[0][0], rest.pop(0)[1]]
    orders = [rest.pop(0), rest.pop(0)] if last else None
    outs = rest
    depth, _, width = pieces[0].shape
    for i in range(depth):
        left = jnp.concatenate([piece[i] for piece in pieces], axis=0)
        for n in range(2):
            right = queries[n][(offset + i) * width:(offset + i + 1) * width, :]
            got = jnp.dot(left, right, preferred_element_type=F32)
            totals[n] = got if totals[n] is None else totals[n] + got
    if not last:
        for n in range(2):
            outs[0][n] = totals[n]
        return
    cols, q_rows = totals[0].shape
    rows = q_rows // len(outs)
    for n in range(2):
        high = totals[n].astype(BF16)
        left = totals[n] - high.astype(F32)
        middle = left.astype(BF16)
        low = (left - middle.astype(F32)).astype(BF16)
        wanted = lax.rem(orders[n][...], q_rows)
        pick = (lax.broadcasted_iota(jnp.int32, (q_rows, q_rows), 0) == wanted).astype(F32).astype(BF16)
        picked = jnp.dot(jnp.concatenate([high, middle, low], axis=0), pick, preferred_element_type=F32)
        picked = picked[:cols] + (picked[cols:2 * cols] + picked[2 * cols:])
        for m, out in enumerate(outs):
            out[:, n * rows:(n + 1) * rows] = picked[:, m * rows:(m + 1) * rows]


def score(parts, queries, offset, pieces, before=None, orders=None):
    _, seqs, width = pieces[0].shape
    q_rows = queries[0].shape[1]
    cols = len(pieces) * seqs
    args = [*queries, *pieces]
    if before is not None:
        args.append(before)
    if orders is None:
        shapes = [jax.ShapeDtypeStruct((2, cols, q_rows), F32)]
    else:
        args += orders
        shapes = [jax.ShapeDtypeStruct((cols, 2 * q_rows // parts), F32)] * parts
    done = pl.pallas_call(
        functools.partial(score_kernel, offset, len(pieces), before is None, orders is not None),
        in_specs=[IN_VMEM] * len(args),
        out_specs=[IN_VMEM] * len(shapes),
        out_shape=shapes,
        compiler_params=PARAMS,
        cost_estimate=FREE,
        name="score",
    )(*args)
    return done[0] if orders is None else done


def reduce_kernel(parts, crossing, seqs, sets, *refs):
    own, other = refs[-2:]
    rows = own.shape[1]
    where = {k: (g, n) for g, ks in enumerate(sets) for n, k in enumerate(ks)}
    size = crossing * seqs
    for k in range(parts):
        total = None
        for m in range(parts):
            g, n = where[k ^ m]
            got = refs[g * parts + m][pl.ds(n * size, size), :]
            total = got if total is None else total + got
        own[pl.ds(k * size, size), :] = total[:, :rows]
        other[pl.ds(k * size, size), :] = total[:, rows:]


def reduce(parts, crossing, seqs, sets, messages):
    flat = [message for group in messages for message in group]
    shape = jax.ShapeDtypeStruct((parts * crossing * seqs, flat[0].shape[1] // 2), F32)
    return pl.pallas_call(
        functools.partial(reduce_kernel, parts, crossing, seqs, sets),
        in_specs=[IN_VMEM] * len(flat),
        out_specs=[IN_VMEM] * 2,
        out_shape=[shape] * 2,
        compiler_params=PARAMS,
        cost_estimate=FREE,
        name="reduce",
    )(*flat)


def finish_kernel(parts, dp, seqs, own, other, out, columns):
    z, d = lax.axis_index("feat"), lax.axis_index("dp")
    crossed = (0, dp // 2)
    for k in range(parts):
        for n, e in enumerate(crossed):
            for flip, ref in ((0, own), (1, other)):
                place = ((d ^ e ^ flip) * parts + (z ^ k)) * seqs
                rows = ref[pl.ds((k * len(crossed) + n) * seqs, seqs), :]
                columns[pl.ds(pl.multiple_of(place, seqs), seqs), :] = rows
    out[...] = columns[...].T


def finish(parts, dp, seqs, own, other):
    rows = own.shape[1]
    total = parts * dp * seqs
    return pl.pallas_call(
        functools.partial(finish_kernel, parts, dp, seqs),
        in_specs=[IN_VMEM] * 2,
        out_specs=IN_VMEM,
        out_shape=jax.ShapeDtypeStruct((rows, total), F32),
        scratch_shapes=[pltpu.VMEM((total, rows), F32)],
        compiler_params=PARAMS,
        cost_estimate=FREE,
        name="finish",
    )(own, other)


def swap(array, axis, size, by):
    return lax.ppermute(array, axis, [(i, i ^ by) for i in range(size)])


def after(array, *earlier):
    return lax.optimization_barrier((array, *earlier))[0]


def direct(parts, dp, layer_in, grad_out, in_proj, out_proj, queries, seq_ids, valid_counts, owner_order):
    seqs = valid_counts.shape[0]
    half = in_proj.shape[1] // parts // 2
    me = lax.axis_index("feat")
    cross = lambda array: swap(array, "dp", dp, dp // 2)
    pair = lambda array: swap(array, "dp", dp, 1)
    move = lambda array, k: swap(array, "feat", parts, k)
    order = jnp.take(owner_order.reshape(parts, -1), me ^ jnp.arange(parts), axis=0).reshape(1, -1)
    orders = [order, pair(order)]
    ask = [(1, 0, 1), (2, 0, 2), (3, 0, 2), (0, 0, 1), (2, 1, 2), (3, 1, 2)]
    g1, g2a, g3a, g0, g2b, g3b = grads(parts, ask, layer_in, grad_out, in_proj, out_proj, seq_ids, valid_counts)
    turned = [turn(queries), turn(pair(queries))]
    x0 = cross(g0)
    z1, z2a, z3a = move(g1, 1), move(g2a, 2), move(g3a, 3)
    z2b, z3b = move(after(g2b, x0), 2), move(after(g3b, x0), 3)
    x1, x2a, x3a, x2b, x3b = map(cross, (z1, z2a, z3a, z2b, z3b))
    near = score(parts, turned, 0, [g0, x0, z1, x1], None, orders)
    part = score(parts, turned, 0, [z2a, x2a, z3a, x3a])
    far = score(parts, turned, half, [z2b, x2b, z3b, x3b], part, orders)
    messages = [[group[0]] + [move(group[m], m) for m in range(1, parts)] for group in (near, far)]
    own, other = reduce(parts, 2, seqs, [[0, 1], [2, 3]], messages)
    return finish(parts, dp, seqs, own, pair(other))


def gathered(parts, dp, layer_in, grad_out, in_proj, out_proj, queries, seq_ids, valid_counts, owner_order):
    ask = [(k, 0, 1) for k in range(parts)]
    own = jnp.stack(grads(parts, ask, layer_in, grad_out, in_proj, out_proj, seq_ids, valid_counts))
    own = jnp.take(own, lax.axis_index("feat") ^ jnp.arange(parts), axis=0)
    size = own.shape[1]
    rows = lax.all_to_all(own, "feat", split_axis=0, concat_axis=0, tiled=True)
    rows = lax.all_gather(rows, "dp", axis=0, tiled=True)
    q_rows = queries.shape[0]
    by_row = queries.reshape(q_rows, size, -1)
    scored = jnp.einsum("qij,gisj->qgs", by_row, rows, preferred_element_type=F32)
    scored = jnp.take(scored.reshape(q_rows, -1), owner_order % q_rows, axis=0)
    return lax.psum_scatter(scored, "feat", scatter_dimension=0, tiled=True)


def solution(mesh):
    parts, dp = mesh.shape["feat"], mesh.shape["dp"]
    in_specs = (
        P(("dom", "dp", "feat"), None),
        P(("dom", "dp", "feat"), None),
        P(),
        P(),
        P(("dom", "dp"), "feat"),
        P(("dom", "dp", "feat"), None),
        P(("dom", "dp", "feat")),
        P(("dom", "dp")),
    )
    out_specs = P(("dom", "dp", "feat"), None)
    body = functools.partial(direct if parts == 4 and dp == 4 else gathered, parts, dp)
    return jax.shard_map(body, mesh=mesh, in_specs=in_specs, out_specs=out_specs, check_vma=False)
```

time: 214 us -> 97.5 us (0.46)
  local copies, waits for them, and re-layouts: 67.9 us -> 0.73 us
  blocking collectives: 54.4 us -> 0 us
  starting transfers between devices: 0.22 us -> 30.1 us
  Pallas kernels: 0 us -> 28 us
  matrix products: 19 us -> 0 us
  waiting for transfers between devices: 56.2 us -> 38.3 us
  between operations: 13.5 us -> 0.13 us
    gather x97 -> x1, local copies, waits for them, and re-layouts: 60.9 us -> 0.56 us  [direct(): jnp.take(owner_order.reshape(parts, -1), me ^ jnp.arange(parts), axis=0)]
    all_to_all x1 -> x0, blocking collectives: 54.4 us -> none  [local(): lax.all_to_all(seq_grads, 'feat', split_axis=1, concat_axis=0, tiled=True)]
    ppermute x0 -> x20, waiting for transfers between devices: none -> 38.3 us  [swap(): return lax.ppermute(array, axis, [(i, i ^ by) for i in range(size)])]
    all_gather x1 -> x0, waiting for transfers between devices: 36.4 us -> none  [local(): lax.all_gather(train_rows, 'dp', axis=0, tiled=True)]
    ppermute x0 -> x20, starting transfers between devices: none -> 30.1 us  [swap(): return lax.ppermute(array, axis, [(i, i ^ by) for i in range(size)])]
    pallas_call x0 -> x8, Pallas kernels: none -> 28 us  [the longest x1 10.5 us: grads(): pl.pallas_call(functools.partial(grads_kernel, parts, ask), in_specs=[IN_...]
    reduce_scatter x1 -> x0, waiting for transfers between devices: 19.8 us -> none  [local(): result = lax.psum_scatter(scored, 'feat', scatter_dimension=0, tiled=True)]
    dot_general x4 -> x0, matrix products: 19 us -> none  [the longest x1 8.84 us: local(): lax.dot_general(ordered, lax.all_gather(train_rows, 'dp', axis=0, tiled=T...]
  transfers between devices with their start and end apart: 2 -> 20, of which waited for: 2 -> 7; matrix products, arithmetic and copies ran while one was open for 10% -> 1% of each run, Pallas kernels for 0% -> 28%
where the time goes in v1:
time: 97.5 us; the launch traced here: 97.4 us
  waiting for transfers between devices  38.3 us (39%)
  starting transfers between devices  30.1 us (31%)
  Pallas kernels  28 us (29%)
    ppermute x20, waiting for transfers between devices, swap(): return lax.ppermute(array, axis, [(i, i ^ by) for i in range(size)])  38.3 us
    ppermute x20, starting transfers between devices, swap(): return lax.ppermute(array, axis, [(i, i ^ by) for i in range(size)])  30.1 us
    pallas_call x1, Pallas kernels, grads(): pl.pallas_call(functools.partial(grads_kernel, parts, ask), in_specs=[IN_...  10.5 us
    pallas_call x3, Pallas kernels, score(): pl.pallas_call(functools.partial(score_kernel, offset, len(pieces), befor...  8.87 us
    pallas_call x2, Pallas kernels, turn(): pl.pallas_call(turn_kernel, in_specs=[IN_HBM], out_specs=IN_VMEM, out_sha...  7.82 us
  transfers between devices with their start and end apart: 20, of which 7 were waited for; matrix products, arithmetic and copies ran while one was open for 1% of the time, Pallas kernels for 28%

profile of v1, /device:TPU:0, one launch (start us, length us, event | category | flops | bytes accessed | tf_op | source)
XLA Modules:
  0.0 97.4 jit_solution(3392866331189410647)
XLA Ops:
  0.0 0.5 collective-permute-start
  0.5 10.5 %sequence_grads.1 = (bf16[64,16,256]{2,1,0:T(8,128)(2,1)S(1)}, bf16[32,16,256]{2,1,0:T(8,128)(2,1)S(1)}, bf16[32,16,256]{2,1,0:T(8,128)(2,1)S(1)}, bf16[64,16,25...) custom-call(bf16[1024,2048]{1,0:T(8,128)(2,1)} %layer.1, bf16[1024,2048]{1,0:T(8,128)(2,1)} %grad.1, ...), custom_call_target="tpu_custom_call" | custom-call | tf_op jit(solution)/shard_map/sequence_grads/pallas_call | solution.py:91
  11.0 2.6 %collective-permute-start.1 = (bf16[64,16,256]{2,1,0:T(8,128)(2,1)S(1)}, bf16[64,16,256]{2,1,0:T(8,128)(2,1)S(1)}, u32[]{:S(2)}, u32[]{:S(2)}) collective-permute-start(bf16[64,16,256]{2,1,0:T(8,128)(2,1)S(1)} %get-tuple-element.23.rest_2_), channel_id=1, source_target_pairs={{0,2},{1,3},{2,0},{3,1},{4,6},{5,7},{6,4},{7,5},{8,10},{9,11},{10,... | collective-permute-start | bytes 1572872 | tf_op jit(solution)/shard_map/ppermute | solution.py:256
  13.5 1.6 %collective-permute-start.2 = (bf16[64,16,256]{2,1,0:T(8,128)(2,1)S(1)}, bf16[64,16,256]{2,1,0:T(8,128)(2,1)S(1)}, u32[]{:S(2)}, u32[]{:S(2)}) collective-permute-start(bf16[64,16,256]{2,1,0:T(8,128)(2,1)S(1)} %get-tuple-element.24), channel_id=1, source_target_pairs={{0,4},{4,0},{8,12},{12,8},{1,5},{5,1},{9,13},{13,9},{2,6},{6,2},{1... | collective-permute-start | bytes 1572872 | tf_op jit(solution)/shard_map/ppermute | solution.py:256
  15.1 2.6 %collective-permute-start.12 = (bf16[32,16,256]{2,1,0:T(8,128)(2,1)S(1)}, bf16[32,16,256]{2,1,0:T(8,128)(2,1)S(1)}, u32[]{:S(2)}, u32[]{:S(2)}) collective-permute-start(bf16[32,16,256]{2,1,0:T(8,128)(2,1)S(1)} %get-tuple-element.33), channel_id=1, source_target_pairs={{0,8},{4,12},{8,0},{12,4},{1,9},{5,13},{9,1},{13,5},{2,10},{6,14},... | collective-permute-start | bytes 786440 | tf_op jit(solution)/shard_map/ppermute | solution.py:256
  17.7 0.2 collective-permute-start.14
  17.9 15.1 %collective-permute-done.12.rest_2_ = bf16[32,16,256]{2,1,0:T(8,128)(2,1)S(1)} collective-permute-done((bf16[32,16,256]{2,1,0:T(8,128)(2,1)S(1)}, bf16[32,16,256]{2,1,0:T(8,128)(2,1)S(1)}, u32[]{:S(2)}, u32[]{:S(2)}) %collective-permute-start.12) | collective-permute-done | bytes 262176 | tf_op jit(solution)/shard_map/ppermute | solution.py:256
  33.0 0.5 collective-permute-start.13
  33.6 0.0 collective-permute-done.1.rest_3_
  33.6 2.5 %collective-permute-start.10 = (bf16[32,16,256]{2,1,0:T(8,128)(2,1)}, bf16[32,16,256]{2,1,0:T(8,128)(2,1)S(1)}, u32[]{:S(2)}, u32[]{:S(2)}) collective-permute-start(bf16[32,16,256]{2,1,0:T(8,128)(2,1)} %get-tuple-element.32), channel_id=1, source_target_pairs={{0,12},{4,8},{8,4},{12,0},{1,13},{5,9},{9,5},{13,1},{2,14},{6,10},... | collective-permute-start | bytes 786440 | tf_op jit(solution)/shard_map/ppermute | solution.py:256
  36.1 5.6 %collective-permute-done.14.rest_4_ = bf16[32,16,256]{2,1,0:T(8,128)(2,1)S(1)} collective-permute-done((bf16[32,16,256]{2,1,0:T(8,128)(2,1)S(1)}, bf16[32,16,256]{2,1,0:T(8,128)(2,1)S(1)}, u32[]{:S(2)}, u32[]{:S(2)}) %collective-permute-start.14) | collective-permute-done | bytes 262176 | tf_op jit(solution)/shard_map/ppermute | solution.py:256
  41.6 7.6 %collective-permute-start.8 = (bf16[32,16,256]{2,1,0:T(8,128)(2,1)}, bf16[32,16,256]{2,1,0:T(8,128)(2,1)S(1)}, u32[]{:S(2)}, u32[]{:S(2)}) collective-permute-start(bf16[32,16,256]{2,1,0:T(8,128)(2,1)} %get-tuple-element.30), channel_id=1, source_target_pairs={{0,8},{4,12},{8,0},{12,4},{1,9},{5,13},{9,1},{13,5},{2,10},{6,14},... | collective-permute-start | bytes 786440 | tf_op jit(solution)/shard_map/ppermute | solution.py:256
  49.2 0.0 collective-permute-done.2.rest_4_
  49.2 0.5 collective-permute-start.3
  49.8 0.0 collective-permute-done.13.rest_3_
  49.8 1.6 %collective-permute-start.15 = (bf16[32,16,256]{2,1,0:T(8,128)(2,1)S(1)}, bf16[32,16,256]{2,1,0:T(8,128)(2,1)}, u32[]{:S(2)}, u32[]{:S(2)}) collective-permute-start(bf16[32,16,256]{2,1,0:T(8,128)(2,1)S(1)} %collective-permute-done.14.rest_4_), channel_id=1, source_target_pairs={{0,2},{1,3},{2,0},{3,1},{4,6},{5,7},{6,4},{7,5},{8,10},{9,11},{10,... | collective-permute-start | bytes 786440 | tf_op jit(solution)/shard_map/ppermute | solution.py:256
  51.4 0.5 collective-permute-start.11
  51.9 11.6 %collective-permute-done.8.rest_2_ = bf16[32,16,256]{2,1,0:T(8,128)(2,1)S(1)} collective-permute-done((bf16[32,16,256]{2,1,0:T(8,128)(2,1)}, bf16[32,16,256]{2,1,0:T(8,128)(2,1)S(1)}, u32[]{:S(2)}, u32[]{:S(2)}) %collective-permute-start.8) | collective-permute-done | bytes 262176 | tf_op jit(solution)/shard_map/ppermute | solution.py:256
  63.5 0.5 collective-permute-start.9
  64.1 0.1 reshape.50
  64.2 0.6 gather_fusion
  64.7 0.1 broadcast_select_fusion
  64.8 0.1 select_n.33.rest_6_.rest_7_
  64.9 0.0 collective-permute-done.source
  64.9 0.0 collective-permute-start.4
  64.9 3.9 %turn.2.rest_0_ = bf16[16384,256]{1,0:T(8,128)(2,1)S(1)} custom-call(bf16[256,16384]{1,0:T(8,128)(2,1)} %source.1), custom_call_target="tpu_custom_call" | custom-call | tf_op jit(solution)/shard_map/turn/pallas_call | solution.py:130
  68.8 3.9 %turn.3.rest_1_ = bf16[16384,256]{1,0:T(8,128)(2,1)S(1)} custom-call(bf16[256,16384]{1,0:T(8,128)(2,1)} %collective-permute-done.source), custom_call_target="tpu_custom_call" | custom-call | tf_op jit(solution)/shard_map/turn/pallas_call | solution.py:130
  72.7 2.7 %score.4.rest_6_ = f32[2,64,256]{2,1,0:T(8,128)S(1)} custom-call(bf16[16384,256]{1,0:T(8,128)(2,1)S(1)} %turn.2.rest_0_, bf16[16384,256]{1,0:T(8,128)(2,1)S(1)} %turn.3.rest_1_, bf16[32,16,256]{2,1,0:T(8,128)(2,1)S(1)} %collective-permute-done.12.rest_2_, bf16[32,16,256]{2,1,0:T(8,128)(2,1)S(1)} %collective-permute-done.13.rest_3_, ...), custom_call_target="tpu_custom_call" | custom-call | tf_op jit(solution)/shard_map/score/pallas_call | solution.py:187
  75.5 0.0 collective-permute-done.11.rest_5_
  75.5 2.4 %collective-permute-done.9.rest_3_ = bf16[32,16,256]{2,1,0:T(8,128)(2,1)} collective-permute-done((bf16[32,16,256]{2,1,0:T(8,128)(2,1)S(1)}, bf16[32,16,256]{2,1,0:T(8,128)(2,1)}, u32[]{:S(2)}, u32[]{:S(2)}) %collective-permute-start.9) | collective-permute-done | bytes 262176 | tf_op jit(solution)/shard_map/ppermute | solution.py:256
  77.9 2.9 %score.5 = (f32[64,128]{1,0:T(8,128)S(1)}, f32[64,128]{1,0:T(8,128)S(1)}, f32[64,128]{1,0:T(8,128)S(1)}, f32[64,128]{1,0:T(8,128)S(1)}) custom-call(bf16[16384,256]{1,0:T(8,128)(2,1)S(1)} %turn.2.rest_0_, bf16[16384,256]{1,0:T(8,128)(2,1)S(1)} %turn.3.rest_1_, bf16[32,16,256]{2,1,0:T(8,128)(2,1)S(1)} %collective-permute-done.8.rest_2_, ...), custom_call_target="tpu_custom_call" | custom-call | tf_op jit(solution)/shard_map/score/pallas_call | solution.py:187
  80.8 0.1 collective-permute-start.16
  80.8 0.6 collective-permute-start.17
  81.5 3.8 %collective-permute-start.18 = (f32[64,128]{1,0:T(8,128)S(1)}, f32[64,128]{1,0:T(8,128)S(1)}, u32[]{:S(2)}, u32[]{:S(2)}) collective-permute-start(f32[64,128]{1,0:T(8,128)S(1)} %get-tuple-element.38), channel_id=1, source_target_pairs={{0,12},{4,8},{8,4},{12,0},{1,13},{5,9},{9,5},{13,1},{2,14},{6,10},... | collective-permute-start | bytes 98312 | tf_op jit(solution)/shard_map/ppermute | solution.py:256
  85.2 3.3 %score.3 = (f32[64,128]{1,0:T(8,128)S(1)}, f32[64,128]{1,0:T(8,128)S(1)}, f32[64,128]{1,0:T(8,128)S(1)}, f32[64,128]{1,0:T(8,128)S(1)}) custom-call(bf16[16384,256]{1,0:T(8,128)(2,1)S(1)} %turn.2.rest_0_, bf16[16384,256]{1,0:T(8,128)(2,1)S(1)} %turn.3.rest_1_, bf16[64,16,256]{2,1,0:T(8,128)(2,1)S(1)} %get-tuple-element.23.rest_2_, ...), custom_call_target="tpu_custom_call" | custom-call | tf_op jit(solution)/shard_map/score/pallas_call | solution.py:187
  88.5 0.1 collective-permute-start.5
  88.6 0.6 collective-permute-start.6
  89.2 0.0 collective-permute-done.16.refs_5_
  89.2 3.8 %collective-permute-start.7 = (f32[64,128]{1,0:T(8,128)S(1)}, f32[64,128]{1,0:T(8,128)S(1)}, u32[]{:S(2)}, u32[]{:S(2)}) collective-permute-start(f32[64,128]{1,0:T(8,128)S(1)} %get-tuple-element.28), channel_id=1, source_target_pairs={{0,12},{4,8},{8,4},{12,0},{1,13},{5,9},{9,5},{13,1},{2,14},{6,10},... | collective-permute-start | bytes 98312 | tf_op jit(solution)/shard_map/ppermute | solution.py:256
  93.0 0.0 collective-permute-done.17.refs_6_
  93.0 0.0 collective-permute-done.18.refs_7_
  93.0 0.0 collective-permute-done.5.refs_1_
  93.0 0.5 collective-permute-done.6.refs_2_
  93.5 1.7 %collective-permute-done.7.refs_3_ = f32[64,128]{1,0:T(8,128)S(1)} collective-permute-done((f32[64,128]{1,0:T(8,128)S(1)}, f32[64,128]{1,0:T(8,128)S(1)}, u32[]{:S(2)}, u32[]{:S(2)}) %collective-permute-start.7) | collective-permute-done | bytes 32800 | tf_op jit(solution)/shard_map/ppermute | solution.py:256
  95.2 0.1 reduce.1
  95.3 0.1 collective-permute-start.19
  95.4 1.2 %collective-permute-done.19.other = f32[128,64]{1,0:T(8,128)S(1)} collective-permute-done((f32[128,64]{1,0:T(8,128)S(1)}, f32[128,64]{1,0:T(8,128)S(1)}, u32[]{:S(2)}, u32[]{:S(2)}) %collective-permute-start.19) | collective-permute-done | bytes 32800 | tf_op jit(solution)/shard_map/ppermute | solution.py:256
  96.6 0.7 finish.1
  (9 shorter events, 0.0 us)
Async XLA Ops:
  0.0 64.1 %copy-start = (s32[256]{0:T(256)S(1)}, s32[256]{0:T(256)}, u32[]{:S(2)}) copy-start(s32[256]{0:T(256)} %param.15) | copy-start | bytes 3076
  0.0 64.9 %collective-permute-start = (bf16[256,16384]{1,0:T(8,128)(2,1)}, bf16[256,16384]{1,0:T(8,128)(2,1)}, u32[]{:S(2)}, u32[]{:S(2)}) collective-permute-start(bf16[256,16384]{1,0:T(8,128)(2,1)} %source.1), channel_id=1, source_target_pairs={{0,1},{1,0},{2,3},{3,2},{4,5},{5,4},{6,7},{7,6},{8,9},{9,8},{10,11... | collective-permute-start | bytes 25165832 | tf_op jit(solution)/shard_map/ppermute | solution.py:256
  11.0 22.6 %collective-permute-start.1 = (bf16[64,16,256]{2,1,0:T(8,128)(2,1)S(1)}, bf16[64,16,256]{2,1,0:T(8,128)(2,1)S(1)}, u32[]{:S(2)}, u32[]{:S(2)}) collective-permute-start(bf16[64,16,256]{2,1,0:T(8,128)(2,1)S(1)} %get-tuple-element.23.rest_2_), channel_id=1, source_target_pairs={{0,2},{1,3},{2,0},{3,1},{4,6},{5,7},{6,4},{7,5},{8,10},{9,11},{10,... | collective-permute-start | bytes 1572872 | tf_op jit(solution)/shard_map/ppermute | solution.py:256
  13.5 35.7 %collective-permute-start.2 = (bf16[64,16,256]{2,1,0:T(8,128)(2,1)S(1)}, bf16[64,16,256]{2,1,0:T(8,128)(2,1)S(1)}, u32[]{:S(2)}, u32[]{:S(2)}) collective-permute-start(bf16[64,16,256]{2,1,0:T(8,128)(2,1)S(1)} %get-tuple-element.24), channel_id=1, source_target_pairs={{0,4},{4,0},{8,12},{12,8},{1,5},{5,1},{9,13},{13,9},{2,6},{6,2},{1... | collective-permute-start | bytes 1572872 | tf_op jit(solution)/shard_map/ppermute | solution.py:256
  15.1 17.9 %collective-permute-start.12 = (bf16[32,16,256]{2,1,0:T(8,128)(2,1)S(1)}, bf16[32,16,256]{2,1,0:T(8,128)(2,1)S(1)}, u32[]{:S(2)}, u32[]{:S(2)}) collective-permute-start(bf16[32,16,256]{2,1,0:T(8,128)(2,1)S(1)} %get-tuple-element.33), channel_id=1, source_target_pairs={{0,8},{4,12},{8,0},{12,4},{1,9},{5,13},{9,1},{13,5},{2,10},{6,14},... | collective-permute-start | bytes 786440 | tf_op jit(solution)/shard_map/ppermute | solution.py:256
  17.7 24.0 %collective-permute-start.14 = (bf16[32,16,256]{2,1,0:T(8,128)(2,1)S(1)}, bf16[32,16,256]{2,1,0:T(8,128)(2,1)S(1)}, u32[]{:S(2)}, u32[]{:S(2)}) collective-permute-start(bf16[32,16,256]{2,1,0:T(8,128)(2,1)S(1)} %get-tuple-element.34), channel_id=1, source_target_pairs={{0,12},{4,8},{8,4},{12,0},{1,13},{5,9},{9,5},{13,1},{2,14},{6,10},... | collective-permute-start | bytes 786440 | tf_op jit(solution)/shard_map/ppermute | solution.py:256
  33.0 16.7 %collective-permute-start.13 = (bf16[32,16,256]{2,1,0:T(8,128)(2,1)S(1)}, bf16[32,16,256]{2,1,0:T(8,128)(2,1)S(1)}, u32[]{:S(2)}, u32[]{:S(2)}) collective-permute-start(bf16[32,16,256]{2,1,0:T(8,128)(2,1)S(1)} %collective-permute-done.12.rest_2_), channel_id=1, source_target_pairs={{0,2},{1,3},{2,0},{3,1},{4,6},{5,7},{6,4},{7,5},{8,10},{9,11},{10,... | collective-permute-start | bytes 786440 | tf_op jit(solution)/shard_map/ppermute | solution.py:256
  33.6 17.8 %collective-permute-start.10 = (bf16[32,16,256]{2,1,0:T(8,128)(2,1)}, bf16[32,16,256]{2,1,0:T(8,128)(2,1)S(1)}, u32[]{:S(2)}, u32[]{:S(2)}) collective-permute-start(bf16[32,16,256]{2,1,0:T(8,128)(2,1)} %get-tuple-element.32), channel_id=1, source_target_pairs={{0,12},{4,8},{8,4},{12,0},{1,13},{5,9},{9,5},{13,1},{2,14},{6,10},... | collective-permute-start | bytes 786440 | tf_op jit(solution)/shard_map/ppermute | solution.py:256
  41.6 21.9 %collective-permute-start.8 = (bf16[32,16,256]{2,1,0:T(8,128)(2,1)}, bf16[32,16,256]{2,1,0:T(8,128)(2,1)S(1)}, u32[]{:S(2)}, u32[]{:S(2)}) collective-permute-start(bf16[32,16,256]{2,1,0:T(8,128)(2,1)} %get-tuple-element.30), channel_id=1, source_target_pairs={{0,8},{4,12},{8,0},{12,4},{1,9},{5,13},{9,1},{13,5},{2,10},{6,14},... | collective-permute-start | bytes 786440 | tf_op jit(solution)/shard_map/ppermute | solution.py:256
  49.2 36.0 %collective-permute-start.3 = (bf16[64,16,256]{2,1,0:T(8,128)(2,1)S(1)}, bf16[64,16,256]{2,1,0:T(8,128)(2,1)S(1)}, u32[]{:S(2)}, u32[]{:S(2)}) collective-permute-start(bf16[64,16,256]{2,1,0:T(8,128)(2,1)S(1)} %collective-permute-done.2.rest_4_), channel_id=1, source_target_pairs={{0,2},{1,3},{2,0},{3,1},{4,6},{5,7},{6,4},{7,5},{8,10},{9,11},{10,... | collective-permute-start | bytes 1572872 | tf_op jit(solution)/shard_map/ppermute | solution.py:256
  49.8 22.9 %collective-permute-start.15 = (bf16[32,16,256]{2,1,0:T(8,128)(2,1)S(1)}, bf16[32,16,256]{2,1,0:T(8,128)(2,1)}, u32[]{:S(2)}, u32[]{:S(2)}) collective-permute-start(bf16[32,16,256]{2,1,0:T(8,128)(2,1)S(1)} %collective-permute-done.14.rest_4_), channel_id=1, source_target_pairs={{0,2},{1,3},{2,0},{3,1},{4,6},{5,7},{6,4},{7,5},{8,10},{9,11},{10,... | collective-permute-start | bytes 786440 | tf_op jit(solution)/shard_map/ppermute | solution.py:256
  51.4 24.1 %collective-permute-start.11 = (bf16[32,16,256]{2,1,0:T(8,128)(2,1)S(1)}, bf16[32,16,256]{2,1,0:T(8,128)(2,1)}, u32[]{:S(2)}, u32[]{:S(2)}) collective-permute-start(bf16[32,16,256]{2,1,0:T(8,128)(2,1)S(1)} %collective-permute-done.10.rest_4_), channel_id=1, source_target_pairs={{0,2},{1,3},{2,0},{3,1},{4,6},{5,7},{6,4},{7,5},{8,10},{9,11},{10,... | collective-permute-start | bytes 786440 | tf_op jit(solution)/shard_map/ppermute | solution.py:256
  63.5 14.4 %collective-permute-start.9 = (bf16[32,16,256]{2,1,0:T(8,128)(2,1)S(1)}, bf16[32,16,256]{2,1,0:T(8,128)(2,1)}, u32[]{:S(2)}, u32[]{:S(2)}) collective-permute-start(bf16[32,16,256]{2,1,0:T(8,128)(2,1)S(1)} %collective-permute-done.8.rest_2_), channel_id=1, source_target_pairs={{0,2},{1,3},{2,0},{3,1},{4,6},{5,7},{6,4},{7,5},{8,10},{9,11},{10,... | collective-permute-start | bytes 786440 | tf_op jit(solution)/shard_map/ppermute | solution.py:256
  64.9 10.6 %collective-permute-start.4 = (s32[1,256]{1,0:T(1,128)S(1)}, s32[1,256]{1,0:T(1,128)S(1)}, u32[]{:S(2)}, u32[]{:S(2)}) collective-permute-start(s32[1,256]{1,0:T(1,128)S(1)} %select_n.33.rest_6_.rest_7_), channel_id=1, source_target_pairs={{0,1},{1,0},{2,3},{3,2},{4,5},{5,4},{6,7},{7,6},{8,9},{9,8},{10,11... | collective-permute-start | bytes 3080 | tf_op jit(solution)/shard_map/ppermute | solution.py:256
  80.8 8.4 %collective-permute-start.16 = (f32[64,128]{1,0:T(8,128)S(1)}, f32[64,128]{1,0:T(8,128)S(1)}, u32[]{:S(2)}, u32[]{:S(2)}) collective-permute-start(f32[64,128]{1,0:T(8,128)S(1)} %get-tuple-element.36), channel_id=1, source_target_pairs={{0,4},{4,0},{8,12},{12,8},{1,5},{5,1},{9,13},{13,9},{2,6},{6,2},{1... | collective-permute-start | bytes 98312 | tf_op jit(solution)/shard_map/ppermute | solution.py:256
  80.8 12.1 %collective-permute-start.17 = (f32[64,128]{1,0:T(8,128)S(1)}, f32[64,128]{1,0:T(8,128)S(1)}, u32[]{:S(2)}, u32[]{:S(2)}) collective-permute-start(f32[64,128]{1,0:T(8,128)S(1)} %get-tuple-element.37), channel_id=1, source_target_pairs={{0,8},{4,12},{8,0},{12,4},{1,9},{5,13},{9,1},{13,5},{2,10},{6,14},... | collective-permute-start | bytes 98312 | tf_op jit(solution)/shard_map/ppermute | solution.py:256
  81.5 11.5 %collective-permute-start.18 = (f32[64,128]{1,0:T(8,128)S(1)}, f32[64,128]{1,0:T(8,128)S(1)}, u32[]{:S(2)}, u32[]{:S(2)}) collective-permute-start(f32[64,128]{1,0:T(8,128)S(1)} %get-tuple-element.38), channel_id=1, source_target_pairs={{0,12},{4,8},{8,4},{12,0},{1,13},{5,9},{9,5},{13,1},{2,14},{6,10},... | collective-permute-start | bytes 98312 | tf_op jit(solution)/shard_map/ppermute | solution.py:256
  88.5 4.5 %collective-permute-start.5 = (f32[64,128]{1,0:T(8,128)S(1)}, f32[64,128]{1,0:T(8,128)S(1)}, u32[]{:S(2)}, u32[]{:S(2)}) collective-permute-start(f32[64,128]{1,0:T(8,128)S(1)} %get-tuple-element.26), channel_id=1, source_target_pairs={{0,4},{4,0},{8,12},{12,8},{1,5},{5,1},{9,13},{13,9},{2,6},{6,2},{1... | collective-permute-start | bytes 98312 | tf_op jit(solution)/shard_map/ppermute | solution.py:256
  88.6 4.9 %collective-permute-start.6 = (f32[64,128]{1,0:T(8,128)S(1)}, f32[64,128]{1,0:T(8,128)S(1)}, u32[]{:S(2)}, u32[]{:S(2)}) collective-permute-start(f32[64,128]{1,0:T(8,128)S(1)} %get-tuple-element.27), channel_id=1, source_target_pairs={{0,8},{4,12},{8,0},{12,4},{1,9},{5,13},{9,1},{13,5},{2,10},{6,14},... | collective-permute-start | bytes 98312 | tf_op jit(solution)/shard_map/ppermute | solution.py:256
  89.2 6.0 %collective-permute-start.7 = (f32[64,128]{1,0:T(8,128)S(1)}, f32[64,128]{1,0:T(8,128)S(1)}, u32[]{:S(2)}, u32[]{:S(2)}) collective-permute-start(f32[64,128]{1,0:T(8,128)S(1)} %get-tuple-element.28), channel_id=1, source_target_pairs={{0,12},{4,8},{8,4},{12,0},{1,13},{5,9},{9,5},{13,1},{2,14},{6,10},... | collective-permute-start | bytes 98312 | tf_op jit(solution)/shard_map/ppermute | solution.py:256
  95.3 1.3 %collective-permute-start.19 = (f32[128,64]{1,0:T(8,128)S(1)}, f32[128,64]{1,0:T(8,128)S(1)}, u32[]{:S(2)}, u32[]{:S(2)}) collective-permute-start(f32[128,64]{1,0:T(8,128)S(1)} %get-tuple-element.40), channel_id=1, source_target_pairs={{0,1},{1,0},{2,3},{3,2},{4,5},{5,4},{6,7},{7,6},{8,9},{9,8},{10,11... | collective-permute-start | bytes 98312 | tf_op jit(solution)/shard_map/ppermute | solution.py:256

commit v2 on v1

--- a/solution.py
+++ b/solution.py
@@ -1,4 +1,5 @@
 import functools
+import math
 
 import jax
 import jax.numpy as jnp
@@ -11,12 +12,15 @@
 BF16 = jnp.bfloat16
 NT = (((1,), (1,)), ((), ()))
 MIB = 1 << 20
-TOKEN_BLOCK = 256
+TOKEN_BLOCK = 512
 ROW_BLOCK = 16
-TURN_BLOCK = 2048
+QUERY_BLOCK = 8
+SPLIT = 4
+QUERY_SLOTS = 8
 FREE = pl.CostEstimate(flops=0, bytes_accessed=0, transcendentals=0)
 IN_HBM = pl.BlockSpec(memory_space=pltpu.HBM)
 IN_VMEM = pl.BlockSpec(memory_space=pltpu.VMEM)
+SMALL = pltpu.CompilerParams(vmem_limit_bytes=6 * MIB)
 PARAMS = pltpu.CompilerParams(vmem_limit_bytes=16 * MIB)
 
 
@@ -43,38 +47,41 @@
     spans = [pl.ds(t, block) for t in range(0, tokens, block)]
     copies = []
 
-    def fetch(source, target):
-        copy = pltpu.make_async_copy(source, target, sems.at[len(copies)])
+    def fetch(source, target, at):
+        copy = pltpu.make_async_copy(source, target, sems.at[at])
         copy.start()
         copies.append(copy)
         return copy
 
-    out_copy = fetch(out_proj, out_v)
-    grad_copies = [fetch(grad.at[spans[0]], grad_v.at[spans[0]])]
-    small_copies = [fetch(ids, ids_v), fetch(valid, valid_v)]
-    grad_copies += [fetch(grad.at[s], grad_v.at[s]) for s in spans[1:]]
-    in_copy = fetch(in_proj, in_v)
-    layer_copies = [fetch(layer.at[s], layer_v.at[s]) for s in spans]
+    out_copy = fetch(out_proj, out_v, 0)
+    grad_copies = [fetch(grad.at[spans[0]], grad_v.at[spans[0]], 4)]
+    small_copies = [fetch(ids, ids_v, 1), fetch(valid, valid_v, 2)]
+    grad_copies += [fetch(grad.at[s], grad_v.at[s], 5 + n) for n, s in enumerate(spans[1:])]
+    in_copy = fetch(in_proj, in_v, 3)
+    layer_copies = [fetch(layer.at[s], layer_v.at[s], 4 + len(spans) + n) for n, s in enumerate(spans)]
     for copy in small_copies:
         copy.wait()
     mask[...] = counted_mask(ids_v[...], valid_v[...])
     out_copy.wait()
-    for s, copy in zip(spans, grad_copies):
-        copy.wait()
+    @pl.loop(0, len(spans))
+    def _(n):
+        s = pl.ds(pl.multiple_of(n * block, block), block)
+        pltpu.make_async_copy(grad.at[s], grad_v.at[s], sems.at[4 + n]).wait()
         out_low[s, :] = jnp.dot(grad_v[s, :], out_v[...], preferred_element_type=F32).astype(BF16)
     in_copy.wait()
-    for s, copy in zip(spans, layer_copies):
-        copy.wait()
+    @pl.loop(0, len(spans))
+    def _(n):
+        s = pl.ds(pl.multiple_of(n * block, block), block)
+        pltpu.make_async_copy(layer.at[s], layer_v.at[s], sems.at[4 + len(spans) + n]).wait()
         low = jnp.dot(layer_v[s, :], in_v[...], preferred_element_type=F32).astype(BF16)
         in_t[:, s] = low.astype(F32).T
     width = in_t.shape[0]
     seqs = mask.shape[0]
     span = width // parts
     me = lax.axis_index("feat")
-    for (k, piece, pieces), out in zip(ask, outs):
-        size = span // pieces
-        small = min(ROW_BLOCK, size)
-        base = pl.multiple_of((me ^ k) * span + piece * size, size)
+    for (k, begin, size), out in zip(ask, outs):
+        small = math.gcd(ROW_BLOCK, size)
+        base = pl.multiple_of((me ^ k) * span + begin, 8)
         for r in range(0, size, small):
             rows = in_t[pl.ds(base + r, small), :]
             left = (rows[:, None, :] * mask[...][None]).astype(BF16).reshape(small * seqs, tokens)
@@ -92,7 +99,7 @@
         functools.partial(grads_kernel, parts, ask),
         in_specs=[IN_HBM] * 6,
         out_specs=[IN_VMEM] * len(ask),
-        out_shape=[pltpu.VMEM((width // parts // part[2], seqs, width), BF16) for part in ask],
+        out_shape=[pltpu.VMEM((size, seqs, width), BF16) for _, _, size in ask],
         scratch_shapes=[
             pltpu.VMEM((tokens, model), BF16),
             pltpu.VMEM((tokens, model), BF16),
@@ -111,89 +118,129 @@
     )(*map(hbm, args))
 
 
-def turn_kernel(source, out, held, sems):
-    depth = source.shape[1]
-    block = min(TURN_BLOCK, depth)
-    copies = []
-    for n, start in enumerate(range(0, depth, block)):
-        span = pl.ds(start, block)
-        copies.append(pltpu.make_async_copy(source.at[:, span], held.at[:, span], sems.at[n]))
-        copies[-1].start()
-    for n, start in enumerate(range(0, depth, block)):
-        copies[n].wait()
-        span = pl.ds(start, block)
-        out[span, :] = held[:, span].T
-
-
-def turn(queries):
-    rows, depth = queries.shape
-    return pl.pallas_call(
-        turn_kernel,
-        in_specs=[IN_HBM],
-        out_specs=IN_VMEM,
-        out_shape=pltpu.VMEM((depth, rows), BF16),
-        scratch_shapes=[pltpu.VMEM((rows, depth), BF16), pltpu.SemaphoreType.DMA((-(-depth // TURN_BLOCK),))],
-        compiler_params=PARAMS,
-        cost_estimate=FREE,
-        name="turn",
-    )(hbm(queries))
-
-
-def score_kernel(offset, count, first, last, *rest):
-    rest = list(rest)
-    queries = [rest.pop(0), rest.pop(0)]
-    pieces = [rest.pop(0) for _ in range(count)]
-    totals = [None, None] if first else [rest[0][0], rest.pop(0)[1]]
-    orders = [rest.pop(0), rest.pop(0)] if last else None
-    outs = rest
-    depth, _, width = pieces[0].shape
-    for i in range(depth):
-        left = jnp.concatenate([piece[i] for piece in pieces], axis=0)
-        for n in range(2):
-            right = queries[n][(offset + i) * width:(offset + i + 1) * width, :]
-            got = jnp.dot(left, right, preferred_element_type=F32)
+def picked(total, order, parts):
+    cols, q_rows = total.shape
+    high = total.astype(BF16)
+    left = total - high.astype(F32)
+    middle = left.astype(BF16)
+    low = (left - middle.astype(F32)).astype(BF16)
+    wanted = lax.rem(order, q_rows)
+    pick = (lax.broadcasted_iota(jnp.int32, (q_rows, q_rows), 0) == wanted).astype(F32).astype(BF16)
+    got = jnp.dot(jnp.concatenate([high, middle, low], axis=0), pick, preferred_element_type=F32)
+    got = got[:cols] + (got[cols:2 * cols] + got[2 * cols:])
+    rows = q_rows // parts
+    return [got[:, m * rows:(m + 1) * rows] for m in range(parts)]
+
+
+def near_kernel(parts, count, own, other, own_order, other_order, *rest):
+    pieces, sent = rest[:count], rest[count:count + parts]
+    turned, held, sems = rest[count + parts:]
+    size, _, width = pieces[0].shape
+    slots, _, span = held.shape
+    block = span // width
+    steps = [(start, n) for start in range(0, size, block) for n in range(2)]
+
+    def fetch(at):
+        start, n = steps[at]
+        source = (own, other)[n].at[:, pl.ds(start * width, span)]
+        copy = pltpu.make_async_copy(source, held.at[at % slots], sems.at[at % slots])
+        copy.start()
+        return copy
+
+    copies = [fetch(at) for at in range(min(slots, len(steps)))]
+    totals = [None, None]
+    for at, (start, n) in enumerate(steps):
+        copies[at].wait()
+        flipped = held[at % slots].T
+        turned[n, pl.ds(start * width, span), :] = flipped
+        for i in range(block):
+            left = jnp.concatenate([piece[start + i] for piece in pieces], axis=0)
+            got = jnp.dot(left, flipped[i * width:(i + 1) * width, :], preferred_element_type=F32)
             totals[n] = got if totals[n] is None else totals[n] + got
-    if not last:
-        for n in range(2):
-            outs[0][n] = totals[n]
-        return
-    cols, q_rows = totals[0].shape
-    rows = q_rows // len(outs)
-    for n in range(2):
-        high = totals[n].astype(BF16)
-        left = totals[n] - high.astype(F32)
-        middle = left.astype(BF16)
-        low = (left - middle.astype(F32)).astype(BF16)
-        wanted = lax.rem(orders[n][...], q_rows)
-        pick = (lax.broadcasted_iota(jnp.int32, (q_rows, q_rows), 0) == wanted).astype(F32).astype(BF16)
-        picked = jnp.dot(jnp.concatenate([high, middle, low], axis=0), pick, preferred_element_type=F32)
-        picked = picked[:cols] + (picked[cols:2 * cols] + picked[2 * cols:])
-        for m, out in enumerate(outs):
-            out[:, n * rows:(n + 1) * rows] = picked[:, m * rows:(m + 1) * rows]
-
-
-def score(parts, queries, offset, pieces, before=None, orders=None):
-    _, seqs, width = pieces[0].shape
-    q_rows = queries[0].shape[1]
+        if at + slots < len(steps):
+            copies.append(fetch(at + slots))
+    rows = sent[0].shape[1] // 2
+    for n, order in enumerate((own_order, other_order)):
+        for out, got in zip(sent, picked(totals[n], order[...], parts)):
+            out[:, n * rows:(n + 1) * rows] = got
+
+
+def near_scores(parts, queries, orders, pieces):
+    size, seqs, width = pieces[0].shape
+    q_rows = queries[0].shape[0]
     cols = len(pieces) * seqs
-    args = [*queries, *pieces]
-    if before is not None:
-        args.append(before)
-    if orders is None:
-        shapes = [jax.ShapeDtypeStruct((2, cols, q_rows), F32)]
-    else:
-        args += orders
-        shapes = [jax.ShapeDtypeStruct((cols, 2 * q_rows // parts), F32)] * parts
+    block = min(QUERY_BLOCK, size)
+    shapes = [jax.ShapeDtypeStruct((cols, 2 * q_rows // parts), F32)] * parts
+    shapes += [pltpu.VMEM((2, size * width, q_rows), BF16)]
     done = pl.pallas_call(
-        functools.partial(score_kernel, offset, len(pieces), before is None, orders is not None),
-        in_specs=[IN_VMEM] * len(args),
+        functools.partial(near_kernel, parts, len(pieces)),
+        in_specs=[IN_HBM] * 2 + [IN_VMEM] * (2 + len(pieces)),
         out_specs=[IN_VMEM] * len(shapes),
         out_shape=shapes,
+        scratch_shapes=[
+            pltpu.VMEM((QUERY_SLOTS, q_rows, block * width), BF16),
+            pltpu.SemaphoreType.DMA((QUERY_SLOTS,)),
+        ],
         compiler_params=PARAMS,
         cost_estimate=FREE,
-        name="score",
+        name="near_scores",
+    )(*map(hbm, queries), *orders, *pieces)
+    return done[:parts], done[parts]
+
+
+def part_kernel(turned, *rest):
+    pieces, out = rest[:-1], rest[-1]
+    size, _, width = pieces[-1].shape
+    for n in range(2):
+        total = None
+        for i in range(size):
+            left = jnp.concatenate([piece[i] for piece in pieces], axis=0)
+            got = jnp.dot(left, turned[n, i * width:(i + 1) * width, :], preferred_element_type=F32)
+            total = got if total is None else total + got
+        out[n] = total
+
+
+def part_scores(turned, pieces):
+    args = [turned, *pieces]
+    return pl.pallas_call(
+        part_kernel,
+        in_specs=[IN_VMEM] * len(args),
+        out_specs=IN_VMEM,
+        out_shape=jax.ShapeDtypeStruct((2, len(pieces) * pieces[0].shape[1], turned.shape[2]), F32),
+        compiler_params=SMALL,
+        cost_estimate=FREE,
+        name="part_scores",
     )(*args)
-    return done[0] if orders is None else done
+
+
+def late_kernel(count, first, turned, before, own_order, other_order, *rest):
+    pieces, sent = rest[:count], rest[count:]
+    size, _, width = pieces[-1].shape
+    totals = [before[0], before[1]]
+    for i in range(size):
+        left = jnp.concatenate([piece[i + first if piece.shape[0] > size else i] for piece in pieces], axis=0)
+        for n in range(2):
+            right = turned[n, (first + i) * width:(first + i + 1) * width, :]
+            totals[n] = totals[n] + jnp.dot(left, right, preferred_element_type=F32)
+    rows = sent[0].shape[1] // 2
+    for n, order in enumerate((own_order, other_order)):
+        for out, got in zip(sent, picked(totals[n], order[...], len(sent))):
+            out[:, n * rows:(n + 1) * rows] = got
+
+
+def late_scores(parts, first, turned, before, orders, pieces):
+    cols, q_rows = before.shape[1:]
+    args = [turned, before, *orders, *pieces]
+    shapes = [jax.ShapeDtypeStruct((cols, 2 * q_rows // parts), F32)] * parts
+    return pl.pallas_call(
+        functools.partial(late_kernel, len(pieces), first),
+        in_specs=[IN_VMEM] * len(args),
+        out_specs=[IN_VMEM] * parts,
+        out_shape=shapes,
+        compiler_params=SMALL,
+        cost_estimate=FREE,
+        name="late_scores",
+    )(*args)
 
 
 def reduce_kernel(parts, crossing, seqs, sets, *refs):
@@ -262,30 +309,38 @@
 
 def direct(parts, dp, layer_in, grad_out, in_proj, out_proj, queries, seq_ids, valid_counts, owner_order):
     seqs = valid_counts.shape[0]
-    half = in_proj.shape[1] // parts // 2
+    span = in_proj.shape[1] // parts
+    cut = span * SPLIT // 8
     me = lax.axis_index("feat")
     cross = lambda array: swap(array, "dp", dp, dp // 2)
     pair = lambda array: swap(array, "dp", dp, 1)
     move = lambda array, k: swap(array, "feat", parts, k)
     order = jnp.take(owner_order.reshape(parts, -1), me ^ jnp.arange(parts), axis=0).reshape(1, -1)
     orders = [order, pair(order)]
-    ask = [(1, 0, 1), (2, 0, 2), (3, 0, 2), (0, 0, 1), (2, 1, 2), (3, 1, 2)]
-    g1, g2a, g3a, g0, g2b, g3b = grads(parts, ask, layer_in, grad_out, in_proj, out_proj, seq_ids, valid_counts)
-    turned = [turn(queries), turn(pair(queries))]
+    ask = [(1, 0, span), (2, 0, span), (3, 0, cut), (0, 0, span), (3, cut, span - cut)]
+    g1, g2, g3a, g0, g3b = grads(parts, ask, layer_in, grad_out, in_proj, out_proj, seq_ids, valid_counts)
+    both = [queries, pair(queries)]
     x0 = cross(g0)
-    z1, z2a, z3a = move(g1, 1), move(g2a, 2), move(g3a, 3)
-    z2b, z3b = move(after(g2b, x0), 2), move(after(g3b, x0), 3)
-    x1, x2a, x3a, x2b, x3b = map(cross, (z1, z2a, z3a, z2b, z3b))
-    near = score(parts, turned, 0, [g0, x0, z1, x1], None, orders)
-    part = score(parts, turned, 0, [z2a, x2a, z3a, x3a])
-    far = score(parts, turned, half, [z2b, x2b, z3b, x3b], part, orders)
-    messages = [[group[0]] + [move(group[m], m) for m in range(1, parts)] for group in (near, far)]
+    z1 = move(g1, 1)
+    z2 = move(g2, 2)
+    z3a = move(g3a, 3)
+    x1 = cross(z1)
+    near, turned = near_scores(parts, both, orders, [g0, x0, z1, x1])
+    z3b = move(after(g3b, x0), 3)
+    x2 = cross(after(z2, x0))
+    x3a = cross(z3a)
+    x3b = cross(after(z3b, near[0]))
+    sent = [near[0]] + [move(near[m], m) for m in range(1, parts)]
+    part = part_scores(turned, [z2, x2, z3a, x3a])
+    far = late_scores(parts, cut, turned, part, orders, [z2, x2, z3b, x3b])
+    messages = [sent, [far[0]] + [move(far[m], m) for m in range(1, parts)]]
     own, other = reduce(parts, 2, seqs, [[0, 1], [2, 3]], messages)
     return finish(parts, dp, seqs, own, pair(other))
 
 
 def gathered(parts, dp, layer_in, grad_out, in_proj, out_proj, queries, seq_ids, valid_counts, owner_order):
-    ask = [(k, 0, 1) for k in range(parts)]
+    span = in_proj.shape[1] // parts
+    ask = [(k, 0, span) for k in range(parts)]
     own = jnp.stack(grads(parts, ask, layer_in, grad_out, in_proj, out_proj, seq_ids, valid_counts))
     own = jnp.take(own, lax.axis_index("feat") ^ jnp.arange(parts), axis=0)
     size = own.shape[1]

time: 97.5 us -> 84 us (0.86)
  Pallas kernels: 28 us -> 19.4 us
  waiting for transfers between devices: 38.3 us -> 31.3 us
  starting transfers between devices: 30.1 us -> 31.5 us
    ppermute x20 -> x18, waiting for transfers between devices: 38.3 us -> 31.3 us  [swap(): return lax.ppermute(array, axis, [(i, i ^ by) for i in range(size)])]
    pallas_call x5 -> x3, Pallas kernels: 16.7 us -> 11.1 us  [the longest x1 7.7 us: near_scores(): pl.pallas_call(functools.partial(near_kernel, parts, len(pieces)), in_spe...]
    pallas_call x1, Pallas kernels: 10.5 us -> 7.47 us  [grads(): pl.pallas_call(functools.partial(grads_kernel, parts, ask), in_specs=[IN_...]
    ppermute x20 -> x18, starting transfers between devices: 30.1 us -> 31.5 us  [swap(): return lax.ppermute(array, axis, [(i, i ^ by) for i in range(size)])]
  transfers between devices with their start and end apart: 20 -> 18, of which waited for: 7 -> 6; matrix products, arithmetic and copies ran while one was open for 1% -> 1% of each run, Pallas kernels for 28% -> 22%
where the time goes in v2:
time: 84 us; the launch traced here: 83.9 us
  starting transfers between devices  31.5 us (38%)
  waiting for transfers between devices  31.3 us (37%)
  Pallas kernels  19.4 us (23%)
  local copies, waits for them, and re-layouts  1.43 us (2%)
    ppermute x18, starting transfers between devices, swap(): return lax.ppermute(array, axis, [(i, i ^ by) for i in range(size)])  31.5 us
    ppermute x18, waiting for transfers between devices, swap(): return lax.ppermute(array, axis, [(i, i ^ by) for i in range(size)])  31.3 us
    pallas_call x1, Pallas kernels, near_scores(): pl.pallas_call(functools.partial(near_kernel, parts, len(pieces)), in_spe...  7.7 us
    pallas_call x1, Pallas kernels, grads(): pl.pallas_call(functools.partial(grads_kernel, parts, ask), in_specs=[IN_...  7.47 us
    pallas_call x1, Pallas kernels, late_scores(): pl.pallas_call(functools.partial(late_kernel, len(pieces), first), in_spe...  1.83 us
  transfers between devices with their start and end apart: 18, of which 6 were waited for; matrix products, arithmetic and copies ran while one was open for 1% of the time, Pallas kernels for 22%

profile of v2, /device:TPU:0, one launch (start us, length us, event | category | flops | bytes accessed | tf_op | source)
XLA Modules:
  0.0 83.9 jit_solution(16695312720536232933)
XLA Ops:
  0.0 0.5 collective-permute-start
  0.5 7.5 %sequence_grads.1 = (bf16[64,16,256]{2,1,0:T(8,128)(2,1)S(1)}, bf16[64,16,256]{2,1,0:T(8,128)(2,1)S(1)}, bf16[32,16,256]{2,1,0:T(8,128)(2,1)S(1)}, bf16[64,16,25...) custom-call(bf16[1024,2048]{1,0:T(8,128)(2,1)} %layer.1, bf16[1024,2048]{1,0:T(8,128)(2,1)} %grad.1, ...), custom_call_target="tpu_custom_call" | custom-call | tf_op jit(solution)/shard_map/sequence_grads/pallas_call | solution.py:98
  7.9 0.0 copy-start
  7.9 0.7 copy-done
  8.6 2.6 %collective-permute-start.3 = (bf16[64,16,256]{2,1,0:T(8,128)(2,1)S(1)}, bf16[64,16,256]{2,1,0:T(8,128)(2,1)S(1)}, u32[]{:S(2)}, u32[]{:S(2)}) collective-permute-start(bf16[64,16,256]{2,1,0:T(8,128)(2,1)S(1)} %get-tuple-element.25), channel_id=1, source_target_pairs={{0,4},{4,0},{8,12},{12,8},{1,5},{5,1},{9,13},{13,9},{2,6},{6,2},{1... | collective-permute-start | bytes 1572872 | tf_op jit(solution)/shard_map/ppermute | solution.py:303
  11.2 1.5 %collective-permute-start.2 = (bf16[64,16,256]{2,1,0:T(8,128)(2,1)S(1)}, bf16[64,16,256]{2,1,0:T(8,128)(2,1)S(1)}, u32[]{:S(2)}, u32[]{:S(2)}) collective-permute-start(bf16[64,16,256]{2,1,0:T(8,128)(2,1)S(1)} %get-tuple-element.24.rest_0_), channel_id=1, source_target_pairs={{0,2},{1,3},{2,0},{3,1},{4,6},{5,7},{6,4},{7,5},{8,10},{9,11},{10,... | collective-permute-start | bytes 1572872 | tf_op jit(solution)/shard_map/ppermute | solution.py:303
  12.7 2.6 %collective-permute-start.8 = (bf16[64,16,256]{2,1,0:T(8,128)(2,1)S(1)}, bf16[64,16,256]{2,1,0:T(8,128)(2,1)S(1)}, u32[]{:S(2)}, u32[]{:S(2)}) collective-permute-start(bf16[64,16,256]{2,1,0:T(8,128)(2,1)S(1)} %get-tuple-element.31), channel_id=1, source_target_pairs={{0,8},{4,12},{8,0},{12,4},{1,9},{5,13},{9,1},{13,5},{2,10},{6,14},... | collective-permute-start | bytes 1572872 | tf_op jit(solution)/shard_map/ppermute | solution.py:303
  15.3 18.4 %collective-permute-done.3.rest_2_ = bf16[64,16,256]{2,1,0:T(8,128)(2,1)S(1)} collective-permute-done((bf16[64,16,256]{2,1,0:T(8,128)(2,1)S(1)}, bf16[64,16,256]{2,1,0:T(8,128)(2,1)S(1)}, u32[]{:S(2)}, u32[]{:S(2)}) %collective-permute-start.3) | collective-permute-done | bytes 524320 | tf_op jit(solution)/shard_map/ppermute | solution.py:303
  33.7 2.6 %collective-permute-start.4 = (bf16[64,16,256]{2,1,0:T(8,128)(2,1)S(1)}, bf16[64,16,256]{2,1,0:T(8,128)(2,1)S(1)}, u32[]{:S(2)}, u32[]{:S(2)}) collective-permute-start(bf16[64,16,256]{2,1,0:T(8,128)(2,1)S(1)} %collective-permute-done.3.rest_2_), channel_id=1, source_target_pairs={{0,2},{1,3},{2,0},{3,1},{4,6},{5,7},{6,4},{7,5},{8,10},{9,11},{10,... | collective-permute-start | bytes 1572872 | tf_op jit(solution)/shard_map/ppermute | solution.py:303
  36.3 0.1 reshape.49
  36.4 0.6 gather_fusion
  37.0 0.1 broadcast_select_fusion
  37.1 0.1 select_n.33.own_order
  37.1 0.0 collective-permute-start.1
  37.2 0.0 collective-permute-done.2.rest_1_
  37.2 2.5 %collective-permute-start.10 = (bf16[32,16,256]{2,1,0:T(8,128)(2,1)}, bf16[32,16,256]{2,1,0:T(8,128)(2,1)S(1)}, u32[]{:S(2)}, u32[]{:S(2)}) collective-permute-start(bf16[32,16,256]{2,1,0:T(8,128)(2,1)} %copy-done), channel_id=1, source_target_pairs={{0,12},{4,8},{8,4},{12,0},{1,13},{5,9},{9,5},{13,1},{2,14},{6,10},... | collective-permute-start | bytes 786440 | tf_op jit(solution)/shard_map/ppermute | solution.py:303
  39.7 0.0 collective-permute-done.8.rest_0_
  39.7 1.5 %collective-permute-start.12 = (bf16[32,16,256]{2,1,0:T(8,128)(2,1)S(1)}, bf16[32,16,256]{2,1,0:T(8,128)(2,1)S(1)}, u32[]{:S(2)}, u32[]{:S(2)}) collective-permute-start(bf16[32,16,256]{2,1,0:T(8,128)(2,1)S(1)} %get-tuple-element.35), channel_id=1, source_target_pairs={{0,12},{4,8},{8,4},{12,0},{1,13},{5,9},{9,5},{13,1},{2,14},{6,10},... | collective-permute-start | bytes 786440 | tf_op jit(solution)/shard_map/ppermute | solution.py:303
  41.1 0.0 collective-permute-done.1.other_order
  41.1 0.5 collective-permute-start.9
  41.7 6.7 %collective-permute-done.10.rest_2_ = bf16[32,16,256]{2,1,0:T(8,128)(2,1)S(1)} collective-permute-done((bf16[32,16,256]{2,1,0:T(8,128)(2,1)}, bf16[32,16,256]{2,1,0:T(8,128)(2,1)S(1)}, u32[]{:S(2)}, u32[]{:S(2)}) %collective-permute-start.10) | collective-permute-done | bytes 262176 | tf_op jit(solution)/shard_map/ppermute | solution.py:303
  48.4 0.0 collective-permute-start.11
  48.4 0.7 collective-permute-done.4.rest_3_
  49.1 0.0 collective-permute-done.other
  49.1 7.7 %near_scores.1 = (f32[64,128]{1,0:T(8,128)S(1)}, f32[64,128]{1,0:T(8,128)S(1)}, f32[64,128]{1,0:T(8,128)S(1)}, f32[64,128]{1,0:T(8,128)S(1)}, bf16[2,16384,256]{2,1,0:T(8,128)(2,1)S(1)}) custom-call(bf16[256,16384]{1,0:T(8,128)(2,1)} %own.1, bf16[256,16384]{1,0:T(8,128)(2,1)} %collective-permute-done.other, s32[1,256]{1,0:T(1,128)S(1)} %select_n.33.own_order, ...), custom_call_target="tpu_custom_call" | custom-call | tf_op jit(solution)/shard_map/near_scores/pallas_call | solution.py:175
  56.8 0.0 collective-permute-done.12.rest_2_
  56.8 2.1 %collective-permute-start.13 = (bf16[32,16,256]{2,1,0:T(8,128)(2,1)S(1)}, bf16[32,16,256]{2,1,0:T(8,128)(2,1)S(1)}, u32[]{:S(2)}, u32[]{:S(2)}) collective-permute-start(bf16[32,16,256]{2,1,0:T(8,128)(2,1)S(1)} %collective-permute-done.12.rest_2_), channel_id=1, source_target_pairs={{0,2},{1,3},{2,0},{3,1},{4,6},{5,7},{6,4},{7,5},{8,10},{9,11},{10,... | collective-permute-start | bytes 786440 | tf_op jit(solution)/shard_map/ppermute | solution.py:303
  58.9 8.2 %collective-permute-start.5 = (f32[64,128]{1,0:T(8,128)S(1)}, f32[64,128]{1,0:T(8,128)S(1)}, u32[]{:S(2)}, u32[]{:S(2)}) collective-permute-start(f32[64,128]{1,0:T(8,128)S(1)} %get-tuple-element.27), channel_id=1, source_target_pairs={{0,4},{4,0},{8,12},{12,8},{1,5},{5,1},{9,13},{13,9},{2,6},{6,2},{1... | collective-permute-start | bytes 98312 | tf_op jit(solution)/shard_map/ppermute | solution.py:303
  67.1 1.0 %collective-permute-start.6 = (f32[64,128]{1,0:T(8,128)S(1)}, f32[64,128]{1,0:T(8,128)S(1)}, u32[]{:S(2)}, u32[]{:S(2)}) collective-permute-start(f32[64,128]{1,0:T(8,128)S(1)} %get-tuple-element.28), channel_id=1, source_target_pairs={{0,8},{4,12},{8,0},{12,4},{1,9},{5,13},{9,1},{13,5},{2,10},{6,14},... | collective-permute-start | bytes 98312 | tf_op jit(solution)/shard_map/ppermute | solution.py:303
  68.1 0.0 collective-permute-done.11.rest_3_
  68.1 1.5 %collective-permute-start.7 = (f32[64,128]{1,0:T(8,128)S(1)}, f32[64,128]{1,0:T(8,128)S(1)}, u32[]{:S(2)}, u32[]{:S(2)}) collective-permute-start(f32[64,128]{1,0:T(8,128)S(1)} %get-tuple-element.29), channel_id=1, source_target_pairs={{0,12},{4,8},{8,4},{12,0},{1,13},{5,9},{9,5},{13,1},{2,14},{6,10},... | collective-permute-start | bytes 98312 | tf_op jit(solution)/shard_map/ppermute | solution.py:303
  69.6 0.0 collective-permute-done.9.rest_1_
  69.6 1.6 %part_scores.1.before = f32[2,64,256]{2,1,0:T(8,128)S(1)} custom-call(bf16[2,16384,256]{2,1,0:T(8,128)(2,1)S(1)} %get-tuple-element.30.turned, bf16[64,16,256]{2,1,0:T(8,128)(2,1)S(1)} %collective-permute-done.8.rest_0_, bf16[64,16,256]{2,1,0:T(8,128)(2,1)S(1)} %collective-permute-done.9.rest_1_, bf16[32,16,256]{2,1,0:T(8,128)(2,1)S(1)} %collective-permute-done.10.rest_2_, ...), custom_call_target="tpu_custom_call" | custom-call | tf_op jit(solution)/shard_map/part_scores/pallas_call | solution.py:205
  71.2 0.0 collective-permute-done.13.rest_3_
  71.2 1.8 %late_scores.1 = (f32[64,128]{1,0:T(8,128)S(1)}, f32[64,128]{1,0:T(8,128)S(1)}, f32[64,128]{1,0:T(8,128)S(1)}, f32[64,128]{1,0:T(8,128)S(1)}) custom-call(bf16[2,16384,256]{2,1,0:T(8,128)(2,1)S(1)} %get-tuple-element.30.turned, f32[2,64,256]{2,1,0:T(8,128)S(1)} %part_scores.1.before, s32[1,256]{1,0:T(1,128)S(1)} %select_n.33.own_order, ...), custom_call_target="tpu_custom_call" | custom-call | tf_op jit(solution)/shard_map/late_scores/pallas_call | solution.py:235
  73.0 1.4 %collective-permute-start.14 = (f32[64,128]{1,0:T(8,128)S(1)}, f32[64,128]{1,0:T(8,128)S(1)}, u32[]{:S(2)}, u32[]{:S(2)}) collective-permute-start(f32[64,128]{1,0:T(8,128)S(1)} %get-tuple-element.38), channel_id=1, source_target_pairs={{0,4},{4,0},{8,12},{12,8},{1,5},{5,1},{9,13},{13,9},{2,6},{6,2},{1... | collective-permute-start | bytes 98312 | tf_op jit(solution)/shard_map/ppermute | solution.py:303
  74.5 1.5 %collective-permute-start.15 = (f32[64,128]{1,0:T(8,128)S(1)}, f32[64,128]{1,0:T(8,128)S(1)}, u32[]{:S(2)}, u32[]{:S(2)}) collective-permute-start(f32[64,128]{1,0:T(8,128)S(1)} %get-tuple-element.39), channel_id=1, source_target_pairs={{0,8},{4,12},{8,0},{12,4},{1,9},{5,13},{9,1},{13,5},{2,10},{6,14},... | collective-permute-start | bytes 98312 | tf_op jit(solution)/shard_map/ppermute | solution.py:303
  76.0 0.0 collective-permute-done.5.refs_1_
  76.0 1.5 %collective-permute-start.16 = (f32[64,128]{1,0:T(8,128)S(1)}, f32[64,128]{1,0:T(8,128)S(1)}, u32[]{:S(2)}, u32[]{:S(2)}) collective-permute-start(f32[64,128]{1,0:T(8,128)S(1)} %get-tuple-element.40), channel_id=1, source_target_pairs={{0,12},{4,8},{8,4},{12,0},{1,13},{5,9},{9,5},{13,1},{2,14},{6,10},... | collective-permute-start | bytes 98312 | tf_op jit(solution)/shard_map/ppermute | solution.py:303
  77.5 0.0 collective-permute-done.6.refs_2_
  77.5 0.0 collective-permute-done.7.refs_3_
  77.5 0.0 collective-permute-done.14.refs_5_
  77.5 2.3 %collective-permute-done.15.refs_6_ = f32[64,128]{1,0:T(8,128)S(1)} collective-permute-done((f32[64,128]{1,0:T(8,128)S(1)}, f32[64,128]{1,0:T(8,128)S(1)}, u32[]{:S(2)}, u32[]{:S(2)}) %collective-permute-start.15) | collective-permute-done | bytes 32800 | tf_op jit(solution)/shard_map/ppermute | solution.py:303
  79.8 1.9 %collective-permute-done.16.refs_7_ = f32[64,128]{1,0:T(8,128)S(1)} collective-permute-done((f32[64,128]{1,0:T(8,128)S(1)}, f32[64,128]{1,0:T(8,128)S(1)}, u32[]{:S(2)}, u32[]{:S(2)}) %collective-permute-start.16) | collective-permute-done | bytes 32800 | tf_op jit(solution)/shard_map/ppermute | solution.py:303
  81.7 0.1 reduce.1
  81.8 0.1 collective-permute-start.17
  81.9 1.2 %collective-permute-done.17.other = f32[128,64]{1,0:T(8,128)S(1)} collective-permute-done((f32[128,64]{1,0:T(8,128)S(1)}, f32[128,64]{1,0:T(8,128)S(1)}, u32[]{:S(2)}, u32[]{:S(2)}) %collective-permute-start.17) | collective-permute-done | bytes 32800 | tf_op jit(solution)/shard_map/ppermute | solution.py:303
  83.1 0.7 finish.1
  (5 shorter events, 0.0 us)
Async XLA Ops:
  0.0 36.3 %copy-start.1 = (s32[256]{0:T(256)S(1)}, s32[256]{0:T(256)}, u32[]{:S(2)}) copy-start(s32[256]{0:T(256)} %param.15) | copy-start | bytes 3076
  0.0 49.1 %collective-permute-start = (bf16[256,16384]{1,0:T(8,128)(2,1)}, bf16[256,16384]{1,0:T(8,128)(2,1)}, u32[]{:S(2)}, u32[]{:S(2)}) collective-permute-start(bf16[256,16384]{1,0:T(8,128)(2,1)} %own.1), channel_id=1, source_target_pairs={{0,1},{1,0},{2,3},{3,2},{4,5},{5,4},{6,7},{7,6},{8,9},{9,8},{10,11... | collective-permute-start | bytes 25165832 | tf_op jit(solution)/shard_map/ppermute | solution.py:303
  7.9 0.7 copy-start
  8.6 25.1 %collective-permute-start.3 = (bf16[64,16,256]{2,1,0:T(8,128)(2,1)S(1)}, bf16[64,16,256]{2,1,0:T(8,128)(2,1)S(1)}, u32[]{:S(2)}, u32[]{:S(2)}) collective-permute-start(bf16[64,16,256]{2,1,0:T(8,128)(2,1)S(1)} %get-tuple-element.25), channel_id=1, source_target_pairs={{0,4},{4,0},{8,12},{12,8},{1,5},{5,1},{9,13},{13,9},{2,6},{6,2},{1... | collective-permute-start | bytes 1572872 | tf_op jit(solution)/shard_map/ppermute | solution.py:303
  11.2 25.9 %collective-permute-start.2 = (bf16[64,16,256]{2,1,0:T(8,128)(2,1)S(1)}, bf16[64,16,256]{2,1,0:T(8,128)(2,1)S(1)}, u32[]{:S(2)}, u32[]{:S(2)}) collective-permute-start(bf16[64,16,256]{2,1,0:T(8,128)(2,1)S(1)} %get-tuple-element.24.rest_0_), channel_id=1, source_target_pairs={{0,2},{1,3},{2,0},{3,1},{4,6},{5,7},{6,4},{7,5},{8,10},{9,11},{10,... | collective-permute-start | bytes 1572872 | tf_op jit(solution)/shard_map/ppermute | solution.py:303
  12.7 27.0 %collective-permute-start.8 = (bf16[64,16,256]{2,1,0:T(8,128)(2,1)S(1)}, bf16[64,16,256]{2,1,0:T(8,128)(2,1)S(1)}, u32[]{:S(2)}, u32[]{:S(2)}) collective-permute-start(bf16[64,16,256]{2,1,0:T(8,128)(2,1)S(1)} %get-tuple-element.31), channel_id=1, source_target_pairs={{0,8},{4,12},{8,0},{12,4},{1,9},{5,13},{9,1},{13,5},{2,10},{6,14},... | collective-permute-start | bytes 1572872 | tf_op jit(solution)/shard_map/ppermute | solution.py:303
  33.7 15.4 %collective-permute-start.4 = (bf16[64,16,256]{2,1,0:T(8,128)(2,1)S(1)}, bf16[64,16,256]{2,1,0:T(8,128)(2,1)S(1)}, u32[]{:S(2)}, u32[]{:S(2)}) collective-permute-start(bf16[64,16,256]{2,1,0:T(8,128)(2,1)S(1)} %collective-permute-done.3.rest_2_), channel_id=1, source_target_pairs={{0,2},{1,3},{2,0},{3,1},{4,6},{5,7},{6,4},{7,5},{8,10},{9,11},{10,... | collective-permute-start | bytes 1572872 | tf_op jit(solution)/shard_map/ppermute | solution.py:303
  37.1 4.0 %collective-permute-start.1 = (s32[1,256]{1,0:T(1,128)S(1)}, s32[1,256]{1,0:T(1,128)S(1)}, u32[]{:S(2)}, u32[]{:S(2)}) collective-permute-start(s32[1,256]{1,0:T(1,128)S(1)} %select_n.33.own_order), channel_id=1, source_target_pairs={{0,1},{1,0},{2,3},{3,2},{4,5},{5,4},{6,7},{7,6},{8,9},{9,8},{10,11... | collective-permute-start | bytes 3080 | tf_op jit(solution)/shard_map/ppermute | solution.py:303
  37.2 11.3 %collective-permute-start.10 = (bf16[32,16,256]{2,1,0:T(8,128)(2,1)}, bf16[32,16,256]{2,1,0:T(8,128)(2,1)S(1)}, u32[]{:S(2)}, u32[]{:S(2)}) collective-permute-start(bf16[32,16,256]{2,1,0:T(8,128)(2,1)} %copy-done), channel_id=1, source_target_pairs={{0,12},{4,8},{8,4},{12,0},{1,13},{5,9},{9,5},{13,1},{2,14},{6,10},... | collective-permute-start | bytes 786440 | tf_op jit(solution)/shard_map/ppermute | solution.py:303
  39.7 17.1 %collective-permute-start.12 = (bf16[32,16,256]{2,1,0:T(8,128)(2,1)S(1)}, bf16[32,16,256]{2,1,0:T(8,128)(2,1)S(1)}, u32[]{:S(2)}, u32[]{:S(2)}) collective-permute-start(bf16[32,16,256]{2,1,0:T(8,128)(2,1)S(1)} %get-tuple-element.35), channel_id=1, source_target_pairs={{0,12},{4,8},{8,4},{12,0},{1,13},{5,9},{9,5},{13,1},{2,14},{6,10},... | collective-permute-start | bytes 786440 | tf_op jit(solution)/shard_map/ppermute | solution.py:303
  41.1 28.4 %collective-permute-start.9 = (bf16[64,16,256]{2,1,0:T(8,128)(2,1)S(1)}, bf16[64,16,256]{2,1,0:T(8,128)(2,1)S(1)}, u32[]{:S(2)}, u32[]{:S(2)}) collective-permute-start(bf16[64,16,256]{2,1,0:T(8,128)(2,1)S(1)} %collective-permute-done.8.rest_0_), channel_id=1, source_target_pairs={{0,2},{1,3},{2,0},{3,1},{4,6},{5,7},{6,4},{7,5},{8,10},{9,11},{10,... | collective-permute-start | bytes 1572872 | tf_op jit(solution)/shard_map/ppermute | solution.py:303
  48.4 19.7 %collective-permute-start.11 = (bf16[32,16,256]{2,1,0:T(8,128)(2,1)S(1)}, bf16[32,16,256]{2,1,0:T(8,128)(2,1)S(1)}, u32[]{:S(2)}, u32[]{:S(2)}) collective-permute-start(bf16[32,16,256]{2,1,0:T(8,128)(2,1)S(1)} %collective-permute-done.10.rest_2_), channel_id=1, source_target_pairs={{0,2},{1,3},{2,0},{3,1},{4,6},{5,7},{6,4},{7,5},{8,10},{9,11},{10,... | collective-permute-start | bytes 786440 | tf_op jit(solution)/shard_map/ppermute | solution.py:303
  56.8 14.3 %collective-permute-start.13 = (bf16[32,16,256]{2,1,0:T(8,128)(2,1)S(1)}, bf16[32,16,256]{2,1,0:T(8,128)(2,1)S(1)}, u32[]{:S(2)}, u32[]{:S(2)}) collective-permute-start(bf16[32,16,256]{2,1,0:T(8,128)(2,1)S(1)} %collective-permute-done.12.rest_2_), channel_id=1, source_target_pairs={{0,2},{1,3},{2,0},{3,1},{4,6},{5,7},{6,4},{7,5},{8,10},{9,11},{10,... | collective-permute-start | bytes 786440 | tf_op jit(solution)/shard_map/ppermute | solution.py:303
  58.9 17.1 %collective-permute-start.5 = (f32[64,128]{1,0:T(8,128)S(1)}, f32[64,128]{1,0:T(8,128)S(1)}, u32[]{:S(2)}, u32[]{:S(2)}) collective-permute-start(f32[64,128]{1,0:T(8,128)S(1)} %get-tuple-element.27), channel_id=1, source_target_pairs={{0,4},{4,0},{8,12},{12,8},{1,5},{5,1},{9,13},{13,9},{2,6},{6,2},{1... | collective-permute-start | bytes 98312 | tf_op jit(solution)/shard_map/ppermute | solution.py:303
  67.1 10.4 %collective-permute-start.6 = (f32[64,128]{1,0:T(8,128)S(1)}, f32[64,128]{1,0:T(8,128)S(1)}, u32[]{:S(2)}, u32[]{:S(2)}) collective-permute-start(f32[64,128]{1,0:T(8,128)S(1)} %get-tuple-element.28), channel_id=1, source_target_pairs={{0,8},{4,12},{8,0},{12,4},{1,9},{5,13},{9,1},{13,5},{2,10},{6,14},... | collective-permute-start | bytes 98312 | tf_op jit(solution)/shard_map/ppermute | solution.py:303
  68.1 9.3 %collective-permute-start.7 = (f32[64,128]{1,0:T(8,128)S(1)}, f32[64,128]{1,0:T(8,128)S(1)}, u32[]{:S(2)}, u32[]{:S(2)}) collective-permute-start(f32[64,128]{1,0:T(8,128)S(1)} %get-tuple-element.29), channel_id=1, source_target_pairs={{0,12},{4,8},{8,4},{12,0},{1,13},{5,9},{9,5},{13,1},{2,14},{6,10},... | collective-permute-start | bytes 98312 | tf_op jit(solution)/shard_map/ppermute | solution.py:303
  73.0 4.5 %collective-permute-start.14 = (f32[64,128]{1,0:T(8,128)S(1)}, f32[64,128]{1,0:T(8,128)S(1)}, u32[]{:S(2)}, u32[]{:S(2)}) collective-permute-start(f32[64,128]{1,0:T(8,128)S(1)} %get-tuple-element.38), channel_id=1, source_target_pairs={{0,4},{4,0},{8,12},{12,8},{1,5},{5,1},{9,13},{13,9},{2,6},{6,2},{1... | collective-permute-start | bytes 98312 | tf_op jit(solution)/shard_map/ppermute | solution.py:303
  74.5 5.3 %collective-permute-start.15 = (f32[64,128]{1,0:T(8,128)S(1)}, f32[64,128]{1,0:T(8,128)S(1)}, u32[]{:S(2)}, u32[]{:S(2)}) collective-permute-start(f32[64,128]{1,0:T(8,128)S(1)} %get-tuple-element.39), channel_id=1, source_target_pairs={{0,8},{4,12},{8,0},{12,4},{1,9},{5,13},{9,1},{13,5},{2,10},{6,14},... | collective-permute-start | bytes 98312 | tf_op jit(solution)/shard_map/ppermute | solution.py:303
  76.0 5.7 %collective-permute-start.16 = (f32[64,128]{1,0:T(8,128)S(1)}, f32[64,128]{1,0:T(8,128)S(1)}, u32[]{:S(2)}, u32[]{:S(2)}) collective-permute-start(f32[64,128]{1,0:T(8,128)S(1)} %get-tuple-element.40), channel_id=1, source_target_pairs={{0,12},{4,8},{8,4},{12,0},{1,13},{5,9},{9,5},{13,1},{2,14},{6,10},... | collective-permute-start | bytes 98312 | tf_op jit(solution)/shard_map/ppermute | solution.py:303
  81.8 1.3 %collective-permute-start.17 = (f32[128,64]{1,0:T(8,128)S(1)}, f32[128,64]{1,0:T(8,128)S(1)}, u32[]{:S(2)}, u32[]{:S(2)}) collective-permute-start(f32[128,64]{1,0:T(8,128)S(1)} %get-tuple-element.42), channel_id=1, source_target_pairs={{0,1},{1,0},{2,3},{3,2},{4,5},{5,4},{6,7},{7,6},{8,9},{9,8},{10,11... | collective-permute-start | bytes 98312 | tf_op jit(solution)/shard_map/ppermute | solution.py:303

commit v3 on v2

--- a/solution.py
+++ b/solution.py
@@ -39,9 +39,24 @@
     return jnp.where((ids == seq) & (position < limit), 1.0, 0.0).astype(F32)
 
 
-def grads_kernel(parts, ask, layer, grad, in_proj, out_proj, ids, valid, *rest):
+def slice_grads(parts, ask, in_t, out_low, mask, outs):
+    width, tokens = in_t.shape
+    seqs = mask.shape[0]
+    span = width // parts
+    me = lax.axis_index("feat")
+    for (k, begin, size), out in zip(ask, outs):
+        small = math.gcd(ROW_BLOCK, size)
+        base = pl.multiple_of((me ^ k) * span + begin, 8)
+        for r in range(0, size, small):
+            rows = in_t[pl.ds(base + r, small), :]
+            left = (rows[:, None, :] * mask[...][None]).astype(BF16).reshape(small * seqs, tokens)
+            got = jnp.dot(left, out_low[...], preferred_element_type=F32).astype(BF16)
+            out[pl.ds(r, small)] = got.reshape(small, seqs, got.shape[1])
+
+
+def project_kernel(parts, ask, layer, grad, in_proj, out_proj, ids, valid, in_t, out_low, mask, *rest):
     outs = rest[: len(ask)]
-    layer_v, grad_v, in_v, out_v, ids_v, valid_v, in_t, out_low, mask, sems = rest[len(ask):]
+    layer_v, grad_v, in_v, out_v, ids_v, valid_v, sems = rest[len(ask):]
     tokens = layer.shape[0]
     block = min(TOKEN_BLOCK, tokens)
     spans = [pl.ds(t, block) for t in range(0, tokens, block)]
@@ -75,31 +90,26 @@
         pltpu.make_async_copy(layer.at[s], layer_v.at[s], sems.at[4 + len(spans) + n]).wait()
         low = jnp.dot(layer_v[s, :], in_v[...], preferred_element_type=F32).astype(BF16)
         in_t[:, s] = low.astype(F32).T
-    width = in_t.shape[0]
-    seqs = mask.shape[0]
-    span = width // parts
-    me = lax.axis_index("feat")
-    for (k, begin, size), out in zip(ask, outs):
-        small = math.gcd(ROW_BLOCK, size)
-        base = pl.multiple_of((me ^ k) * span + begin, 8)
-        for r in range(0, size, small):
-            rows = in_t[pl.ds(base + r, small), :]
-            left = (rows[:, None, :] * mask[...][None]).astype(BF16).reshape(small * seqs, tokens)
-            got = jnp.dot(left, out_low[...], preferred_element_type=F32).astype(BF16)
-            out[pl.ds(r, small)] = got.reshape(small, seqs, got.shape[1])
-
-
-def grads(parts, ask, layer_in, grad_out, in_proj, out_proj, seq_ids, valid_counts):
+    slice_grads(parts, ask, in_t, out_low, mask, outs)
+
+
+def piece_shapes(ask, seqs, width):
+    return [(pltpu.HBM if late else pltpu.VMEM)((size, seqs, width), BF16) for _, _, size, late in ask]
+
+
+def project(parts, ask, layer_in, grad_out, in_proj, out_proj, seq_ids, valid_counts):
     tokens, model = layer_in.shape
     width = in_proj.shape[1]
     seqs = valid_counts.shape[0]
     block = min(TOKEN_BLOCK, tokens)
     args = (layer_in, grad_out, in_proj, out_proj, seq_ids, valid_counts.reshape(1, seqs))
-    return pl.pallas_call(
-        functools.partial(grads_kernel, parts, ask),
+    shapes = [pltpu.VMEM((width, tokens), F32), pltpu.VMEM((tokens, width), BF16), pltpu.VMEM((seqs, tokens), F32)]
+    shapes += piece_shapes(ask, seqs, width)
+    done = pl.pallas_call(
+        functools.partial(project_kernel, parts, [part[:3] for part in ask]),
         in_specs=[IN_HBM] * 6,
-        out_specs=[IN_VMEM] * len(ask),
-        out_shape=[pltpu.VMEM((size, seqs, width), BF16) for _, _, size in ask],
+        out_specs=[IN_VMEM] * len(shapes),
+        out_shape=shapes,
         scratch_shapes=[
             pltpu.VMEM((tokens, model), BF16),
             pltpu.VMEM((tokens, model), BF16),
@@ -107,15 +117,30 @@
             pltpu.VMEM((model, width), BF16),
             pltpu.VMEM((1, tokens), jnp.int32),
             pltpu.VMEM((1, seqs), jnp.int32),
-            pltpu.VMEM((width, tokens), F32),
-            pltpu.VMEM((tokens, width), BF16),
-            pltpu.VMEM((seqs, tokens), F32),
             pltpu.SemaphoreType.DMA((4 + 2 * (tokens // block),)),
         ],
         compiler_params=PARAMS,
         cost_estimate=FREE,
+        name="project",
+    )(*map(hbm, args))
+    return done[:3], done[3:]
+
+
+def grads_kernel(parts, ask, in_t, out_low, mask, *outs):
+    slice_grads(parts, ask, in_t, out_low, mask, outs)
+
+
+def grads(parts, ask, in_t, out_low, mask):
+    tokens, width = out_low.shape
+    return pl.pallas_call(
+        functools.partial(grads_kernel, parts, [part[:3] for part in ask]),
+        in_specs=[IN_VMEM] * 3,
+        out_specs=[IN_VMEM] * len(ask),
+        out_shape=piece_shapes(ask, mask.shape[0], width),
+        compiler_params=SMALL,
+        cost_estimate=FREE,
         name="sequence_grads",
-    )(*map(hbm, args))
+    )(in_t, out_low, mask)
 
 
 def picked(total, order, parts):
@@ -246,16 +271,17 @@
 def reduce_kernel(parts, crossing, seqs, sets, *refs):
     own, other = refs[-2:]
     rows = own.shape[1]
-    where = {k: (g, n) for g, ks in enumerate(sets) for n, k in enumerate(ks)}
-    size = crossing * seqs
+    where = {key: (g, n) for g, keys in enumerate(sets) for n, key in enumerate(keys)}
     for k in range(parts):
-        total = None
-        for m in range(parts):
-            g, n = where[k ^ m]
-            got = refs[g * parts + m][pl.ds(n * size, size), :]
-            total = got if total is None else total + got
-        own[pl.ds(k * size, size), :] = total[:, :rows]
-        other[pl.ds(k * size, size), :] = total[:, rows:]
+        for e in range(crossing):
+            total = None
+            for m in range(parts):
+                g, n = where[k ^ m, e]
+                got = refs[g * parts + m][pl.ds(n * seqs, seqs), :]
+                total = got if total is None else total + got
+            place = pl.ds((k * crossing + e) * seqs, seqs)
+            own[place, :] = total[:, :rows]
+            other[place, :] = total[:, rows:]
 
 
 def reduce(parts, crossing, seqs, sets, messages):
@@ -317,31 +343,36 @@
     move = lambda array, k: swap(array, "feat", parts, k)
     order = jnp.take(owner_order.reshape(parts, -1), me ^ jnp.arange(parts), axis=0).reshape(1, -1)
     orders = [order, pair(order)]
-    ask = [(1, 0, span), (2, 0, span), (3, 0, cut), (0, 0, span), (3, cut, span - cut)]
-    g1, g2, g3a, g0, g3b = grads(parts, ask, layer_in, grad_out, in_proj, out_proj, seq_ids, valid_counts)
+    low, (g2, g1) = project(
+        parts, [(2, 0, span, False), (1, 0, span, False)], layer_in, grad_out, in_proj, out_proj, seq_ids, valid_counts
+    )
+    g0, g3a, g3b = grads(parts, [(0, 0, span, False), (3, 0, cut, False), (3, cut, span - cut, True)], *low)
     both = [queries, pair(queries)]
     x0 = cross(g0)
     z1 = move(g1, 1)
     z2 = move(g2, 2)
-    z3a = move(g3a, 3)
-    x1 = cross(z1)
-    near, turned = near_scores(parts, both, orders, [g0, x0, z1, x1])
-    z3b = move(after(g3b, x0), 3)
-    x2 = cross(after(z2, x0))
-    x3a = cross(z3a)
-    x3b = cross(after(z3b, near[0]))
+    z3a = move(after(g3a, z1), 3)
+    x1p = cross(g1)
+    x1 = move(after(x1p, z1), 1)
+    near, turned = near_scores(parts, both, orders, [g0, x0, z1, z2])
+    z3b = move(after(g3b, z2), 3)
+    x2 = cross(z2)
+    x3a = cross(after(z3a, near[0]))
+    x3b = cross(z3b)
     sent = [near[0]] + [move(near[m], m) for m in range(1, parts)]
-    part = part_scores(turned, [z2, x2, z3a, x3a])
-    far = late_scores(parts, cut, turned, part, orders, [z2, x2, z3b, x3b])
+    part = part_scores(turned, [x1, x2, z3a, x3a])
+    far = late_scores(parts, cut, turned, part, orders, [x1, x2, z3b, x3b])
     messages = [sent, [far[0]] + [move(far[m], m) for m in range(1, parts)]]
-    own, other = reduce(parts, 2, seqs, [[0, 1], [2, 3]], messages)
+    sets = [[(0, 0), (0, 1), (1, 0), (2, 0)], [(1, 1), (2, 1), (3, 0), (3, 1)]]
+    own, other = reduce(parts, 2, seqs, sets, messages)
     return finish(parts, dp, seqs, own, pair(other))
 
 
 def gathered(parts, dp, layer_in, grad_out, in_proj, out_proj, queries, seq_ids, valid_counts, owner_order):
     span = in_proj.shape[1] // parts
-    ask = [(k, 0, span) for k in range(parts)]
-    own = jnp.stack(grads(parts, ask, layer_in, grad_out, in_proj, out_proj, seq_ids, valid_counts))
+    ask = [(k, 0, span, False) for k in range(parts)]
+    _, own = project(parts, ask, layer_in, grad_out, in_proj, out_proj, seq_ids, valid_counts)
+    own = jnp.stack(own)
     own = jnp.take(own, lax.axis_index("feat") ^ jnp.arange(parts), axis=0)
     size = own.shape[1]
     rows = lax.all_to_all(own, "feat", split_axis=0, concat_axis=0, tiled=True)

time: 84 us -> 81.6 us (0.971)
  starting transfers between devices: 31.5 us -> 27.3 us
  waiting for transfers between devices: 31.3 us -> 33 us
  Pallas kernels: 19.4 us -> 20.3 us
    ppermute x18 -> x19, starting transfers between devices: 31.5 us -> 27.3 us  [swap(): return lax.ppermute(array, axis, [(i, i ^ by) for i in range(size)])]
    ppermute x18 -> x19, waiting for transfers between devices: 31.3 us -> 33 us  [swap(): return lax.ppermute(array, axis, [(i, i ^ by) for i in range(size)])]
    pallas_call x1 -> x2, Pallas kernels: 7.47 us -> 8.37 us  [the longest x1 6.39 us: project(): pl.pallas_call(functools.partial(project_kernel, parts, [part[:3] for par...]
  transfers between devices with their start and end apart: 18 -> 19, of which waited for: 6 -> 6; matrix products, arithmetic and copies ran while one was open for 1% -> 1% of each run, Pallas kernels for 22% -> 24%
where the time goes in v3:
time: 81.6 us; the launch traced here: 81.5 us
  waiting for transfers between devices  33 us (40%)
  starting transfers between devices  27.3 us (33%)
  Pallas kernels  20.3 us (25%)
    ppermute x19, waiting for transfers between devices, swap(): return lax.ppermute(array, axis, [(i, i ^ by) for i in range(size)])  33 us
    ppermute x19, starting transfers between devices, swap(): return lax.ppermute(array, axis, [(i, i ^ by) for i in range(size)])  27.3 us
    pallas_call x1, Pallas kernels, near_scores(): pl.pallas_call(functools.partial(near_kernel, parts, len(pieces)), in_spe...  7.69 us
    pallas_call x1, Pallas kernels, project(): pl.pallas_call(functools.partial(project_kernel, parts, [part[:3] for par...  6.39 us
    pallas_call x1, Pallas kernels, grads(): pl.pallas_call(functools.partial(grads_kernel, parts, [part[:3] for part...  1.98 us
    pallas_call x1, Pallas kernels, late_scores(): pl.pallas_call(functools.partial(late_kernel, len(pieces), first), in_spe...  1.83 us
  transfers between devices with their start and end apart: 19, of which 6 were waited for; matrix products, arithmetic and copies ran while one was open for 1% of the time, Pallas kernels for 24%

profile of v3, /device:TPU:0, one launch (start us, length us, event | category | flops | bytes accessed | tf_op | source)
XLA Modules:
  0.0 81.5 jit_solution(16375485937847770392)
XLA Ops:
  0.0 0.5 collective-permute-start
  0.5 6.4 %project.1 = (f32[256,1024]{1,0:T(8,128)S(1)}, bf16[1024,256]{1,0:T(8,128)(2,1)S(1)}, f32[16,1024]{1,0:T(8,128)S(1)}, bf16[64,16,256]{2,1,0:T(8,128)(2,1)S(1)}, bf16[64,16,256]{2,1,0:T(8,128)(2,1)S(1)}) custom-call(bf16[1024,2048]{1,0:T(8,128)(2,1)} %layer.1, bf16[1024,2048]{1,0:T(8,128)(2,1)} %grad.1, bf16[2048,256]{1,0:T(8,128)(2,1)} %in_proj.1, ...), custom_call_target="tpu_custom_call" | custom-call | tf_op jit(solution)/shard_map/project/pallas_call | solution.py:108
  6.9 2.7 %collective-permute-start.3 = (bf16[64,16,256]{2,1,0:T(8,128)(2,1)S(1)}, bf16[64,16,256]{2,1,0:T(8,128)(2,1)S(1)}, u32[]{:S(2)}, u32[]{:S(2)}) collective-permute-start(bf16[64,16,256]{2,1,0:T(8,128)(2,1)S(1)} %get-tuple-element.32), channel_id=1, source_target_pairs={{0,4},{4,0},{8,12},{12,8},{1,5},{5,1},{9,13},{13,9},{2,6},{6,2},{1... | collective-permute-start | bytes 1572872 | tf_op jit(solution)/shard_map/ppermute | solution.py:329
  9.5 1.5 %collective-permute-start.8 = (bf16[64,16,256]{2,1,0:T(8,128)(2,1)S(1)}, bf16[64,16,256]{2,1,0:T(8,128)(2,1)}, u32[]{:S(2)}, u32[]{:S(2)}) collective-permute-start(bf16[64,16,256]{2,1,0:T(8,128)(2,1)S(1)} %get-tuple-element.32), channel_id=1, source_target_pairs={{0,2},{1,3},{2,0},{3,1},{4,6},{5,7},{6,4},{7,5},{8,10},{9,11},{10,... | collective-permute-start | bytes 1572872 | tf_op jit(solution)/shard_map/ppermute | solution.py:329
  11.0 2.0 %sequence_grads.1 = (bf16[64,16,256]{2,1,0:T(8,128)(2,1)S(1)}, bf16[32,16,256]{2,1,0:T(8,128)(2,1)S(1)}, bf16[32,16,256]{2,1,0:T(8,128)(2,1)}) custom-call(f32[256,1024]{1,0:T(8,128)S(1)} %get-tuple-element.28.in_t, bf16[1024,256]{1,0:T(8,128)(2,1)S(1)} %get-tuple-element.29.out_low, f32[16,1024]{1,0:T(8,128)S(1)} %get-tuple-element.30.mask), custom_call_target="tpu_custom_call" | custom-call | tf_op jit(solution)/shard_map/sequence_grads/pallas_call | solution.py:135
  13.0 0.5 collective-permute-start.2
  13.5 2.6 %collective-permute-start.4 = (bf16[64,16,256]{2,1,0:T(8,128)(2,1)S(1)}, bf16[64,16,256]{2,1,0:T(8,128)(2,1)S(1)}, u32[]{:S(2)}, u32[]{:S(2)}) collective-permute-start(bf16[64,16,256]{2,1,0:T(8,128)(2,1)S(1)} %get-tuple-element.33), channel_id=1, source_target_pairs={{0,8},{4,12},{8,0},{12,4},{1,9},{5,13},{9,1},{13,5},{2,10},{6,14},... | collective-permute-start | bytes 1572872 | tf_op jit(solution)/shard_map/ppermute | solution.py:329
  16.1 0.1 reshape.49
  16.2 0.6 gather_fusion
  16.8 0.1 broadcast_select_fusion
  16.8 0.1 select_n.33.own_order
  16.9 12.8 %collective-permute-done.3.rest_2_ = bf16[64,16,256]{2,1,0:T(8,128)(2,1)S(1)} collective-permute-done((bf16[64,16,256]{2,1,0:T(8,128)(2,1)S(1)}, bf16[64,16,256]{2,1,0:T(8,128)(2,1)S(1)}, u32[]{:S(2)}, u32[]{:S(2)}) %collective-permute-start.3) | collective-permute-done | bytes 524320 | tf_op jit(solution)/shard_map/ppermute | solution.py:329
  29.8 0.0 collective-permute-start.1
  29.8 0.0 collective-permute-done.8
  29.8 2.6 %collective-permute-start.11 = (bf16[32,16,256]{2,1,0:T(8,128)(2,1)S(1)}, bf16[32,16,256]{2,1,0:T(8,128)(2,1)S(1)}, u32[]{:S(2)}, u32[]{:S(2)}) collective-permute-start(bf16[32,16,256]{2,1,0:T(8,128)(2,1)S(1)} %get-tuple-element.41), channel_id=1, source_target_pairs={{0,12},{4,8},{8,4},{12,0},{1,13},{5,9},{9,5},{13,1},{2,14},{6,10},... | collective-permute-start | bytes 786440 | tf_op jit(solution)/shard_map/ppermute | solution.py:329
  32.4 0.0 collective-permute-done.1.other_order
  32.4 0.0 collective-permute-start.9
  32.4 13.7 %collective-permute-done.4.rest_3_ = bf16[64,16,256]{2,1,0:T(8,128)(2,1)S(1)} collective-permute-done((bf16[64,16,256]{2,1,0:T(8,128)(2,1)S(1)}, bf16[64,16,256]{2,1,0:T(8,128)(2,1)S(1)}, u32[]{:S(2)}, u32[]{:S(2)}) %collective-permute-start.4) | collective-permute-done | bytes 524320 | tf_op jit(solution)/shard_map/ppermute | solution.py:329
  46.2 1.5 %collective-permute-start.10 = (bf16[64,16,256]{2,1,0:T(8,128)(2,1)S(1)}, bf16[64,16,256]{2,1,0:T(8,128)(2,1)S(1)}, u32[]{:S(2)}, u32[]{:S(2)}) collective-permute-start(bf16[64,16,256]{2,1,0:T(8,128)(2,1)S(1)} %collective-permute-done.4.rest_3_), channel_id=1, source_target_pairs={{0,2},{1,3},{2,0},{3,1},{4,6},{5,7},{6,4},{7,5},{8,10},{9,11},{10,... | collective-permute-start | bytes 1572872 | tf_op jit(solution)/shard_map/ppermute | solution.py:329
  47.6 0.0 collective-permute-done.2.rest_1_
  47.7 2.5 %collective-permute-start.13 = (bf16[32,16,256]{2,1,0:T(8,128)(2,1)}, bf16[32,16,256]{2,1,0:T(8,128)(2,1)S(1)}, u32[]{:S(2)}, u32[]{:S(2)}) collective-permute-start(bf16[32,16,256]{2,1,0:T(8,128)(2,1)} %get-tuple-element.44), channel_id=1, source_target_pairs={{0,12},{4,8},{8,4},{12,0},{1,13},{5,9},{9,5},{13,1},{2,14},{6,10},... | collective-permute-start | bytes 786440 | tf_op jit(solution)/shard_map/ppermute | solution.py:329
  50.1 0.0 collective-permute-done.other
  50.1 7.7 %near_scores.1 = (f32[64,128]{1,0:T(8,128)S(1)}, f32[64,128]{1,0:T(8,128)S(1)}, f32[64,128]{1,0:T(8,128)S(1)}, f32[64,128]{1,0:T(8,128)S(1)}, bf16[2,16384,256]{2,1,0:T(8,128)(2,1)S(1)}) custom-call(bf16[256,16384]{1,0:T(8,128)(2,1)} %own.1, bf16[256,16384]{1,0:T(8,128)(2,1)} %collective-permute-done.other, s32[1,256]{1,0:T(1,128)S(1)} %select_n.33.own_order, ...), custom_call_target="tpu_custom_call" | custom-call | tf_op jit(solution)/shard_map/near_scores/pallas_call | solution.py:200
  57.8 0.0 collective-permute-done.11.rest_2_
  57.8 0.6 collective-permute-start.12
  58.4 0.0 collective-permute-done.13.rest_2_
  58.4 1.5 %collective-permute-start.14 = (bf16[32,16,256]{2,1,0:T(8,128)(2,1)S(1)}, bf16[32,16,256]{2,1,0:T(8,128)(2,1)S(1)}, u32[]{:S(2)}, u32[]{:S(2)}) collective-permute-start(bf16[32,16,256]{2,1,0:T(8,128)(2,1)S(1)} %collective-permute-done.13.rest_2_), channel_id=1, source_target_pairs={{0,2},{1,3},{2,0},{3,1},{4,6},{5,7},{6,4},{7,5},{8,10},{9,11},{10,... | collective-permute-start | bytes 786440 | tf_op jit(solution)/shard_map/ppermute | solution.py:329
  59.9 3.8 %collective-permute-start.5 = (f32[64,128]{1,0:T(8,128)S(1)}, f32[64,128]{1,0:T(8,128)S(1)}, u32[]{:S(2)}, u32[]{:S(2)}) collective-permute-start(f32[64,128]{1,0:T(8,128)S(1)} %get-tuple-element.35), channel_id=1, source_target_pairs={{0,4},{4,0},{8,12},{12,8},{1,5},{5,1},{9,13},{13,9},{2,6},{6,2},{1... | collective-permute-start | bytes 98312 | tf_op jit(solution)/shard_map/ppermute | solution.py:329
  63.8 0.0 collective-permute-done.9.rest_0_
  63.8 1.0 %collective-permute-start.6 = (f32[64,128]{1,0:T(8,128)S(1)}, f32[64,128]{1,0:T(8,128)S(1)}, u32[]{:S(2)}, u32[]{:S(2)}) collective-permute-start(f32[64,128]{1,0:T(8,128)S(1)} %get-tuple-element.36), channel_id=1, source_target_pairs={{0,8},{4,12},{8,0},{12,4},{1,9},{5,13},{9,1},{13,5},{2,10},{6,14},... | collective-permute-start | bytes 98312 | tf_op jit(solution)/shard_map/ppermute | solution.py:329
  64.8 0.0 collective-permute-done.10.rest_1_
  64.8 1.5 %collective-permute-start.7 = (f32[64,128]{1,0:T(8,128)S(1)}, f32[64,128]{1,0:T(8,128)S(1)}, u32[]{:S(2)}, u32[]{:S(2)}) collective-permute-start(f32[64,128]{1,0:T(8,128)S(1)} %get-tuple-element.37), channel_id=1, source_target_pairs={{0,12},{4,8},{8,4},{12,0},{1,13},{5,9},{9,5},{13,1},{2,14},{6,10},... | collective-permute-start | bytes 98312 | tf_op jit(solution)/shard_map/ppermute | solution.py:329
  66.3 0.0 collective-permute-done.12.rest_3_
  66.3 1.6 %part_scores.1.before = f32[2,64,256]{2,1,0:T(8,128)S(1)} custom-call(bf16[2,16384,256]{2,1,0:T(8,128)(2,1)S(1)} %get-tuple-element.38.turned, bf16[64,16,256]{2,1,0:T(8,128)(2,1)S(1)} %collective-permute-done.9.rest_0_, bf16[64,16,256]{2,1,0:T(8,128)(2,1)S(1)} %collective-permute-done.10.rest_1_, bf16[32,16,256]{2,1,0:T(8,128)(2,1)S(1)} %collective-permute-done.11.rest_2_, ...), custom_call_target="tpu_custom_call" | custom-call | tf_op jit(solution)/shard_map/part_scores/pallas_call | solution.py:230
  67.9 0.8 collective-permute-done.14.rest_3_
  68.7 1.8 %late_scores.1 = (f32[64,128]{1,0:T(8,128)S(1)}, f32[64,128]{1,0:T(8,128)S(1)}, f32[64,128]{1,0:T(8,128)S(1)}, f32[64,128]{1,0:T(8,128)S(1)}) custom-call(bf16[2,16384,256]{2,1,0:T(8,128)(2,1)S(1)} %get-tuple-element.38.turned, f32[2,64,256]{2,1,0:T(8,128)S(1)} %part_scores.1.before, s32[1,256]{1,0:T(1,128)S(1)} %select_n.33.own_order, ...), custom_call_target="tpu_custom_call" | custom-call | tf_op jit(solution)/shard_map/late_scores/pallas_call | solution.py:260
  70.5 0.6 collective-permute-start.15
  71.2 2.5 %collective-permute-start.16 = (f32[64,128]{1,0:T(8,128)S(1)}, f32[64,128]{1,0:T(8,128)S(1)}, u32[]{:S(2)}, u32[]{:S(2)}) collective-permute-start(f32[64,128]{1,0:T(8,128)S(1)} %get-tuple-element.47), channel_id=1, source_target_pairs={{0,8},{4,12},{8,0},{12,4},{1,9},{5,13},{9,1},{13,5},{2,10},{6,14},... | collective-permute-start | bytes 98312 | tf_op jit(solution)/shard_map/ppermute | solution.py:329
  73.6 0.0 collective-permute-done.5.refs_1_
  73.6 1.3 %collective-permute-start.17 = (f32[64,128]{1,0:T(8,128)S(1)}, f32[64,128]{1,0:T(8,128)S(1)}, u32[]{:S(2)}, u32[]{:S(2)}) collective-permute-start(f32[64,128]{1,0:T(8,128)S(1)} %get-tuple-element.48), channel_id=1, source_target_pairs={{0,12},{4,8},{8,4},{12,0},{1,13},{5,9},{9,5},{13,1},{2,14},{6,10},... | collective-permute-start | bytes 98312 | tf_op jit(solution)/shard_map/ppermute | solution.py:329
  75.0 0.0 collective-permute-done.6.refs_2_
  75.0 0.0 collective-permute-done.7.refs_3_
  75.0 1.0 %collective-permute-done.16.refs_6_ = f32[64,128]{1,0:T(8,128)S(1)} collective-permute-done((f32[64,128]{1,0:T(8,128)S(1)}, f32[64,128]{1,0:T(8,128)S(1)}, u32[]{:S(2)}, u32[]{:S(2)}) %collective-permute-start.16) | collective-permute-done | bytes 32800 | tf_op jit(solution)/shard_map/ppermute | solution.py:329
  76.0 3.4 %collective-permute-done.17.refs_7_ = f32[64,128]{1,0:T(8,128)S(1)} collective-permute-done((f32[64,128]{1,0:T(8,128)S(1)}, f32[64,128]{1,0:T(8,128)S(1)}, u32[]{:S(2)}, u32[]{:S(2)}) %collective-permute-start.17) | collective-permute-done | bytes 32800 | tf_op jit(solution)/shard_map/ppermute | solution.py:329
  79.4 0.1 reduce.1
  79.5 0.1 collective-permute-start.18
  79.5 1.2 %collective-permute-done.18.other = f32[128,64]{1,0:T(8,128)S(1)} collective-permute-done((f32[128,64]{1,0:T(8,128)S(1)}, f32[128,64]{1,0:T(8,128)S(1)}, u32[]{:S(2)}, u32[]{:S(2)}) %collective-permute-start.18) | collective-permute-done | bytes 32800 | tf_op jit(solution)/shard_map/ppermute | solution.py:329
  80.8 0.7 finish.1
  (6 shorter events, 0.0 us)
Async XLA Ops:
  0.0 16.1 %copy-start = (s32[256]{0:T(256)S(1)}, s32[256]{0:T(256)}, u32[]{:S(2)}) copy-start(s32[256]{0:T(256)} %param.15) | copy-start | bytes 3076
  0.0 50.1 %collective-permute-start = (bf16[256,16384]{1,0:T(8,128)(2,1)}, bf16[256,16384]{1,0:T(8,128)(2,1)}, u32[]{:S(2)}, u32[]{:S(2)}) collective-permute-start(bf16[256,16384]{1,0:T(8,128)(2,1)} %own.1), channel_id=1, source_target_pairs={{0,1},{1,0},{2,3},{3,2},{4,5},{5,4},{6,7},{7,6},{8,9},{9,8},{10,11... | collective-permute-start | bytes 25165832 | tf_op jit(solution)/shard_map/ppermute | solution.py:329
  6.9 22.9 %collective-permute-start.3 = (bf16[64,16,256]{2,1,0:T(8,128)(2,1)S(1)}, bf16[64,16,256]{2,1,0:T(8,128)(2,1)S(1)}, u32[]{:S(2)}, u32[]{:S(2)}) collective-permute-start(bf16[64,16,256]{2,1,0:T(8,128)(2,1)S(1)} %get-tuple-element.32), channel_id=1, source_target_pairs={{0,4},{4,0},{8,12},{12,8},{1,5},{5,1},{9,13},{13,9},{2,6},{6,2},{1... | collective-permute-start | bytes 1572872 | tf_op jit(solution)/shard_map/ppermute | solution.py:329
  9.5 20.3 %collective-permute-start.8 = (bf16[64,16,256]{2,1,0:T(8,128)(2,1)S(1)}, bf16[64,16,256]{2,1,0:T(8,128)(2,1)}, u32[]{:S(2)}, u32[]{:S(2)}) collective-permute-start(bf16[64,16,256]{2,1,0:T(8,128)(2,1)S(1)} %get-tuple-element.32), channel_id=1, source_target_pairs={{0,2},{1,3},{2,0},{3,1},{4,6},{5,7},{6,4},{7,5},{8,10},{9,11},{10,... | collective-permute-start | bytes 1572872 | tf_op jit(solution)/shard_map/ppermute | solution.py:329
  13.0 34.7 %collective-permute-start.2 = (bf16[64,16,256]{2,1,0:T(8,128)(2,1)S(1)}, bf16[64,16,256]{2,1,0:T(8,128)(2,1)S(1)}, u32[]{:S(2)}, u32[]{:S(2)}) collective-permute-start(bf16[64,16,256]{2,1,0:T(8,128)(2,1)S(1)} %get-tuple-element.31.rest_0_), channel_id=1, source_target_pairs={{0,2},{1,3},{2,0},{3,1},{4,6},{5,7},{6,4},{7,5},{8,10},{9,11},{10,... | collective-permute-start | bytes 1572872 | tf_op jit(solution)/shard_map/ppermute | solution.py:329
  13.5 32.6 %collective-permute-start.4 = (bf16[64,16,256]{2,1,0:T(8,128)(2,1)S(1)}, bf16[64,16,256]{2,1,0:T(8,128)(2,1)S(1)}, u32[]{:S(2)}, u32[]{:S(2)}) collective-permute-start(bf16[64,16,256]{2,1,0:T(8,128)(2,1)S(1)} %get-tuple-element.33), channel_id=1, source_target_pairs={{0,8},{4,12},{8,0},{12,4},{1,9},{5,13},{9,1},{13,5},{2,10},{6,14},... | collective-permute-start | bytes 1572872 | tf_op jit(solution)/shard_map/ppermute | solution.py:329
  29.8 2.6 %collective-permute-start.1 = (s32[1,256]{1,0:T(1,128)S(1)}, s32[1,256]{1,0:T(1,128)S(1)}, u32[]{:S(2)}, u32[]{:S(2)}) collective-permute-start(s32[1,256]{1,0:T(1,128)S(1)} %select_n.33.own_order), channel_id=1, source_target_pairs={{0,1},{1,0},{2,3},{3,2},{4,5},{5,4},{6,7},{7,6},{8,9},{9,8},{10,11... | collective-permute-start | bytes 3080 | tf_op jit(solution)/shard_map/ppermute | solution.py:329
  29.8 28.1 %collective-permute-start.11 = (bf16[32,16,256]{2,1,0:T(8,128)(2,1)S(1)}, bf16[32,16,256]{2,1,0:T(8,128)(2,1)S(1)}, u32[]{:S(2)}, u32[]{:S(2)}) collective-permute-start(bf16[32,16,256]{2,1,0:T(8,128)(2,1)S(1)} %get-tuple-element.41), channel_id=1, source_target_pairs={{0,12},{4,8},{8,4},{12,0},{1,13},{5,9},{9,5},{13,1},{2,14},{6,10},... | collective-permute-start | bytes 786440 | tf_op jit(solution)/shard_map/ppermute | solution.py:329
  32.4 31.3 %collective-permute-start.9 = (bf16[64,16,256]{2,1,0:T(8,128)(2,1)}, bf16[64,16,256]{2,1,0:T(8,128)(2,1)S(1)}, u32[]{:S(2)}, u32[]{:S(2)}) collective-permute-start(bf16[64,16,256]{2,1,0:T(8,128)(2,1)} %collective-permute-done.8), channel_id=1, source_target_pairs={{0,4},{4,0},{8,12},{12,8},{1,5},{5,1},{9,13},{13,9},{2,6},{6,2},{1... | collective-permute-start | bytes 1572872 | tf_op jit(solution)/shard_map/ppermute | solution.py:329
  46.2 18.6 %collective-permute-start.10 = (bf16[64,16,256]{2,1,0:T(8,128)(2,1)S(1)}, bf16[64,16,256]{2,1,0:T(8,128)(2,1)S(1)}, u32[]{:S(2)}, u32[]{:S(2)}) collective-permute-start(bf16[64,16,256]{2,1,0:T(8,128)(2,1)S(1)} %collective-permute-done.4.rest_3_), channel_id=1, source_target_pairs={{0,2},{1,3},{2,0},{3,1},{4,6},{5,7},{6,4},{7,5},{8,10},{9,11},{10,... | collective-permute-start | bytes 1572872 | tf_op jit(solution)/shard_map/ppermute | solution.py:329
  47.7 10.8 %collective-permute-start.13 = (bf16[32,16,256]{2,1,0:T(8,128)(2,1)}, bf16[32,16,256]{2,1,0:T(8,128)(2,1)S(1)}, u32[]{:S(2)}, u32[]{:S(2)}) collective-permute-start(bf16[32,16,256]{2,1,0:T(8,128)(2,1)} %get-tuple-element.44), channel_id=1, source_target_pairs={{0,12},{4,8},{8,4},{12,0},{1,13},{5,9},{9,5},{13,1},{2,14},{6,10},... | collective-permute-start | bytes 786440 | tf_op jit(solution)/shard_map/ppermute | solution.py:329
  57.8 8.5 %collective-permute-start.12 = (bf16[32,16,256]{2,1,0:T(8,128)(2,1)S(1)}, bf16[32,16,256]{2,1,0:T(8,128)(2,1)S(1)}, u32[]{:S(2)}, u32[]{:S(2)}) collective-permute-start(bf16[32,16,256]{2,1,0:T(8,128)(2,1)S(1)} %collective-permute-done.11.rest_2_), channel_id=1, source_target_pairs={{0,2},{1,3},{2,0},{3,1},{4,6},{5,7},{6,4},{7,5},{8,10},{9,11},{10,... | collective-permute-start | bytes 786440 | tf_op jit(solution)/shard_map/ppermute | solution.py:329
  58.4 10.2 %collective-permute-start.14 = (bf16[32,16,256]{2,1,0:T(8,128)(2,1)S(1)}, bf16[32,16,256]{2,1,0:T(8,128)(2,1)S(1)}, u32[]{:S(2)}, u32[]{:S(2)}) collective-permute-start(bf16[32,16,256]{2,1,0:T(8,128)(2,1)S(1)} %collective-permute-done.13.rest_2_), channel_id=1, source_target_pairs={{0,2},{1,3},{2,0},{3,1},{4,6},{5,7},{6,4},{7,5},{8,10},{9,11},{10,... | collective-permute-start | bytes 786440 | tf_op jit(solution)/shard_map/ppermute | solution.py:329
  59.9 13.7 %collective-permute-start.5 = (f32[64,128]{1,0:T(8,128)S(1)}, f32[64,128]{1,0:T(8,128)S(1)}, u32[]{:S(2)}, u32[]{:S(2)}) collective-permute-start(f32[64,128]{1,0:T(8,128)S(1)} %get-tuple-element.35), channel_id=1, source_target_pairs={{0,4},{4,0},{8,12},{12,8},{1,5},{5,1},{9,13},{13,9},{2,6},{6,2},{1... | collective-permute-start | bytes 98312 | tf_op jit(solution)/shard_map/ppermute | solution.py:329
  63.8 11.2 %collective-permute-start.6 = (f32[64,128]{1,0:T(8,128)S(1)}, f32[64,128]{1,0:T(8,128)S(1)}, u32[]{:S(2)}, u32[]{:S(2)}) collective-permute-start(f32[64,128]{1,0:T(8,128)S(1)} %get-tuple-element.36), channel_id=1, source_target_pairs={{0,8},{4,12},{8,0},{12,4},{1,9},{5,13},{9,1},{13,5},{2,10},{6,14},... | collective-permute-start | bytes 98312 | tf_op jit(solution)/shard_map/ppermute | solution.py:329
  64.8 10.2 %collective-permute-start.7 = (f32[64,128]{1,0:T(8,128)S(1)}, f32[64,128]{1,0:T(8,128)S(1)}, u32[]{:S(2)}, u32[]{:S(2)}) collective-permute-start(f32[64,128]{1,0:T(8,128)S(1)} %get-tuple-element.37), channel_id=1, source_target_pairs={{0,12},{4,8},{8,4},{12,0},{1,13},{5,9},{9,5},{13,1},{2,14},{6,10},... | collective-permute-start | bytes 98312 | tf_op jit(solution)/shard_map/ppermute | solution.py:329
  70.5 4.5 %collective-permute-start.15 = (f32[64,128]{1,0:T(8,128)S(1)}, f32[64,128]{1,0:T(8,128)S(1)}, u32[]{:S(2)}, u32[]{:S(2)}) collective-permute-start(f32[64,128]{1,0:T(8,128)S(1)} %get-tuple-element.46), channel_id=1, source_target_pairs={{0,4},{4,0},{8,12},{12,8},{1,5},{5,1},{9,13},{13,9},{2,6},{6,2},{1... | collective-permute-start | bytes 98312 | tf_op jit(solution)/shard_map/ppermute | solution.py:329
  71.2 4.8 %collective-permute-start.16 = (f32[64,128]{1,0:T(8,128)S(1)}, f32[64,128]{1,0:T(8,128)S(1)}, u32[]{:S(2)}, u32[]{:S(2)}) collective-permute-start(f32[64,128]{1,0:T(8,128)S(1)} %get-tuple-element.47), channel_id=1, source_target_pairs={{0,8},{4,12},{8,0},{12,4},{1,9},{5,13},{9,1},{13,5},{2,10},{6,14},... | collective-permute-start | bytes 98312 | tf_op jit(solution)/shard_map/ppermute | solution.py:329
  73.6 5.7 %collective-permute-start.17 = (f32[64,128]{1,0:T(8,128)S(1)}, f32[64,128]{1,0:T(8,128)S(1)}, u32[]{:S(2)}, u32[]{:S(2)}) collective-permute-start(f32[64,128]{1,0:T(8,128)S(1)} %get-tuple-element.48), channel_id=1, source_target_pairs={{0,12},{4,8},{8,4},{12,0},{1,13},{5,9},{9,5},{13,1},{2,14},{6,10},... | collective-permute-start | bytes 98312 | tf_op jit(solution)/shard_map/ppermute | solution.py:329
  79.5 1.3 %collective-permute-start.18 = (f32[128,64]{1,0:T(8,128)S(1)}, f32[128,64]{1,0:T(8,128)S(1)}, u32[]{:S(2)}, u32[]{:S(2)}) collective-permute-start(f32[128,64]{1,0:T(8,128)S(1)} %get-tuple-element.50), channel_id=1, source_target_pairs={{0,1},{1,0},{2,3},{3,2},{4,5},{5,4},{6,7},{7,6},{8,9},{9,8},{10,11... | collective-permute-start | bytes 98312 | tf_op jit(solution)/shard_map/ppermute | solution.py:329

commit v4 on v3

--- a/solution.py
+++ b/solution.py
@@ -347,7 +347,7 @@
         parts, [(2, 0, span, False), (1, 0, span, False)], layer_in, grad_out, in_proj, out_proj, seq_ids, valid_counts
     )
     g0, g3a, g3b = grads(parts, [(0, 0, span, False), (3, 0, cut, False), (3, cut, span - cut, True)], *low)
-    both = [queries, pair(queries)]
+    both = [queries, pair(after(queries, g1))]
     x0 = cross(g0)
     z1 = move(g1, 1)
     z2 = move(g2, 2)
@@ -355,7 +355,7 @@
     x1p = cross(g1)
     x1 = move(after(x1p, z1), 1)
     near, turned = near_scores(parts, both, orders, [g0, x0, z1, z2])
-    z3b = move(after(g3b, z2), 3)
+    z3b = move(after(g3b, z1), 3)
     x2 = cross(z2)
     x3a = cross(after(z3a, near[0]))
     x3b = cross(z3b)

time: 81.6 us -> 81.6 us (level)
  transfers between devices with their start and end apart: 19 -> 19, of which waited for: 6 -> 6; matrix products, arithmetic and copies ran while one was open for 1% -> 1% of each run, Pallas kernels for 24% -> 16%
where the time goes in v4:
time: 81.6 us; the launch traced here: 81.5 us
  waiting for transfers between devices  32.9 us (40%)
  starting transfers between devices  27.3 us (33%)
  Pallas kernels  20.3 us (25%)
    ppermute x19, waiting for transfers between devices, swap(): return lax.ppermute(array, axis, [(i, i ^ by) for i in range(size)])  32.9 us
    ppermute x19, starting transfers between devices, swap(): return lax.ppermute(array, axis, [(i, i ^ by) for i in range(size)])  27.3 us
    pallas_call x1, Pallas kernels, near_scores(): pl.pallas_call(functools.partial(near_kernel, parts, len(pieces)), in_spe...  7.69 us
    pallas_call x1, Pallas kernels, project(): pl.pallas_call(functools.partial(project_kernel, parts, [part[:3] for par...  6.41 us
    pallas_call x1, Pallas kernels, grads(): pl.pallas_call(functools.partial(grads_kernel, parts, [part[:3] for part...  1.98 us
    pallas_call x1, Pallas kernels, late_scores(): pl.pallas_call(functools.partial(late_kernel, len(pieces), first), in_spe...  1.83 us
  transfers between devices with their start and end apart: 19, of which 6 were waited for; matrix products, arithmetic and copies ran while one was open for 1% of the time, Pallas kernels for 16%

profile of v4, /device:TPU:0, one launch (start us, length us, event | category | flops | bytes accessed | tf_op | source)
XLA Modules:
  0.0 81.5 jit_solution(8494765030804658877)
XLA Ops:
  0.0 6.4 %project.1 = (f32[256,1024]{1,0:T(8,128)S(1)}, bf16[1024,256]{1,0:T(8,128)(2,1)S(1)}, f32[16,1024]{1,0:T(8,128)S(1)}, bf16[64,16,256]{2,1,0:T(8,128)(2,1)S(1)}, bf16[64,16,256]{2,1,0:T(8,128)(2,1)S(1)}) custom-call(bf16[1024,2048]{1,0:T(8,128)(2,1)} %layer.1, bf16[1024,2048]{1,0:T(8,128)(2,1)} %grad.1, bf16[2048,256]{1,0:T(8,128)(2,1)} %in_proj.1, ...), custom_call_target="tpu_custom_call" | custom-call | tf_op jit(solution)/shard_map/project/pallas_call | solution.py:108
  6.4 0.5 collective-permute-start
  6.9 2.7 %collective-permute-start.3 = (bf16[64,16,256]{2,1,0:T(8,128)(2,1)S(1)}, bf16[64,16,256]{2,1,0:T(8,128)(2,1)S(1)}, u32[]{:S(2)}, u32[]{:S(2)}) collective-permute-start(bf16[64,16,256]{2,1,0:T(8,128)(2,1)S(1)} %get-tuple-element.29), channel_id=1, source_target_pairs={{0,4},{4,0},{8,12},{12,8},{1,5},{5,1},{9,13},{13,9},{2,6},{6,2},{1... | collective-permute-start | bytes 1572872 | tf_op jit(solution)/shard_map/ppermute | solution.py:329
  9.6 1.5 %collective-permute-start.8 = (bf16[64,16,256]{2,1,0:T(8,128)(2,1)S(1)}, bf16[64,16,256]{2,1,0:T(8,128)(2,1)}, u32[]{:S(2)}, u32[]{:S(2)}) collective-permute-start(bf16[64,16,256]{2,1,0:T(8,128)(2,1)S(1)} %get-tuple-element.29), channel_id=1, source_target_pairs={{0,2},{1,3},{2,0},{3,1},{4,6},{5,7},{6,4},{7,5},{8,10},{9,11},{10,... | collective-permute-start | bytes 1572872 | tf_op jit(solution)/shard_map/ppermute | solution.py:329
  11.1 2.0 %sequence_grads.1 = (bf16[64,16,256]{2,1,0:T(8,128)(2,1)S(1)}, bf16[32,16,256]{2,1,0:T(8,128)(2,1)S(1)}, bf16[32,16,256]{2,1,0:T(8,128)(2,1)}) custom-call(f32[256,1024]{1,0:T(8,128)S(1)} %get-tuple-element.31.in_t, bf16[1024,256]{1,0:T(8,128)(2,1)S(1)} %get-tuple-element.32.out_low, f32[16,1024]{1,0:T(8,128)S(1)} %get-tuple-element.33.mask), custom_call_target="tpu_custom_call" | custom-call | tf_op jit(solution)/shard_map/sequence_grads/pallas_call | solution.py:135
  13.1 0.5 collective-permute-start.2
  13.6 2.6 %collective-permute-start.4 = (bf16[64,16,256]{2,1,0:T(8,128)(2,1)S(1)}, bf16[64,16,256]{2,1,0:T(8,128)(2,1)S(1)}, u32[]{:S(2)}, u32[]{:S(2)}) collective-permute-start(bf16[64,16,256]{2,1,0:T(8,128)(2,1)S(1)} %get-tuple-element.35), channel_id=1, source_target_pairs={{0,8},{4,12},{8,0},{12,4},{1,9},{5,13},{9,1},{13,5},{2,10},{6,14},... | collective-permute-start | bytes 1572872 | tf_op jit(solution)/shard_map/ppermute | solution.py:329
  16.2 0.1 reshape.50
  16.3 0.6 gather_fusion
  16.8 0.1 broadcast_select_fusion
  16.9 0.1 select_n.33.own_order
  17.0 12.8 %collective-permute-done.3.rest_2_ = bf16[64,16,256]{2,1,0:T(8,128)(2,1)S(1)} collective-permute-done((bf16[64,16,256]{2,1,0:T(8,128)(2,1)S(1)}, bf16[64,16,256]{2,1,0:T(8,128)(2,1)S(1)}, u32[]{:S(2)}, u32[]{:S(2)}) %collective-permute-start.3) | collective-permute-done | bytes 524320 | tf_op jit(solution)/shard_map/ppermute | solution.py:329
  29.8 0.0 collective-permute-start.1
  29.8 0.0 collective-permute-done.8
  29.8 2.7 %collective-permute-start.11 = (bf16[32,16,256]{2,1,0:T(8,128)(2,1)S(1)}, bf16[32,16,256]{2,1,0:T(8,128)(2,1)S(1)}, u32[]{:S(2)}, u32[]{:S(2)}) collective-permute-start(bf16[32,16,256]{2,1,0:T(8,128)(2,1)S(1)} %get-tuple-element.43), channel_id=1, source_target_pairs={{0,12},{4,8},{8,4},{12,0},{1,13},{5,9},{9,5},{13,1},{2,14},{6,10},... | collective-permute-start | bytes 786440 | tf_op jit(solution)/shard_map/ppermute | solution.py:329
  32.4 0.0 collective-permute-done.1.other_order
  32.5 0.0 collective-permute-start.9
  32.5 13.8 %collective-permute-done.4.rest_3_ = bf16[64,16,256]{2,1,0:T(8,128)(2,1)S(1)} collective-permute-done((bf16[64,16,256]{2,1,0:T(8,128)(2,1)S(1)}, bf16[64,16,256]{2,1,0:T(8,128)(2,1)S(1)}, u32[]{:S(2)}, u32[]{:S(2)}) %collective-permute-start.4) | collective-permute-done | bytes 524320 | tf_op jit(solution)/shard_map/ppermute | solution.py:329
  46.2 1.5 %collective-permute-start.10 = (bf16[64,16,256]{2,1,0:T(8,128)(2,1)S(1)}, bf16[64,16,256]{2,1,0:T(8,128)(2,1)S(1)}, u32[]{:S(2)}, u32[]{:S(2)}) collective-permute-start(bf16[64,16,256]{2,1,0:T(8,128)(2,1)S(1)} %collective-permute-done.4.rest_3_), channel_id=1, source_target_pairs={{0,2},{1,3},{2,0},{3,1},{4,6},{5,7},{6,4},{7,5},{8,10},{9,11},{10,... | collective-permute-start | bytes 1572872 | tf_op jit(solution)/shard_map/ppermute | solution.py:329
  47.7 0.0 collective-permute-done.2.rest_1_
  47.7 2.5 %collective-permute-start.13 = (bf16[32,16,256]{2,1,0:T(8,128)(2,1)}, bf16[32,16,256]{2,1,0:T(8,128)(2,1)S(1)}, u32[]{:S(2)}, u32[]{:S(2)}) collective-permute-start(bf16[32,16,256]{2,1,0:T(8,128)(2,1)} %get-tuple-element.46), channel_id=1, source_target_pairs={{0,12},{4,8},{8,4},{12,0},{1,13},{5,9},{9,5},{13,1},{2,14},{6,10},... | collective-permute-start | bytes 786440 | tf_op jit(solution)/shard_map/ppermute | solution.py:329
  50.2 0.0 collective-permute-done.other
  50.2 7.7 %near_scores.1 = (f32[64,128]{1,0:T(8,128)S(1)}, f32[64,128]{1,0:T(8,128)S(1)}, f32[64,128]{1,0:T(8,128)S(1)}, f32[64,128]{1,0:T(8,128)S(1)}, bf16[2,16384,256]{2,1,0:T(8,128)(2,1)S(1)}) custom-call(bf16[256,16384]{1,0:T(8,128)(2,1)} %own.1, bf16[256,16384]{1,0:T(8,128)(2,1)} %collective-permute-done.other, s32[1,256]{1,0:T(1,128)S(1)} %select_n.33.own_order, ...), custom_call_target="tpu_custom_call" | custom-call | tf_op jit(solution)/shard_map/near_scores/pallas_call | solution.py:200
  57.9 0.0 collective-permute-done.11.rest_2_
  57.9 0.6 collective-permute-start.12
  58.5 0.0 collective-permute-done.13.rest_2_
  58.5 1.5 %collective-permute-start.14 = (bf16[32,16,256]{2,1,0:T(8,128)(2,1)S(1)}, bf16[32,16,256]{2,1,0:T(8,128)(2,1)S(1)}, u32[]{:S(2)}, u32[]{:S(2)}) collective-permute-start(bf16[32,16,256]{2,1,0:T(8,128)(2,1)S(1)} %collective-permute-done.13.rest_2_), channel_id=1, source_target_pairs={{0,2},{1,3},{2,0},{3,1},{4,6},{5,7},{6,4},{7,5},{8,10},{9,11},{10,... | collective-permute-start | bytes 786440 | tf_op jit(solution)/shard_map/ppermute | solution.py:329
  60.0 3.8 %collective-permute-start.5 = (f32[64,128]{1,0:T(8,128)S(1)}, f32[64,128]{1,0:T(8,128)S(1)}, u32[]{:S(2)}, u32[]{:S(2)}) collective-permute-start(f32[64,128]{1,0:T(8,128)S(1)} %get-tuple-element.37), channel_id=1, source_target_pairs={{0,4},{4,0},{8,12},{12,8},{1,5},{5,1},{9,13},{13,9},{2,6},{6,2},{1... | collective-permute-start | bytes 98312 | tf_op jit(solution)/shard_map/ppermute | solution.py:329
  63.8 0.0 collective-permute-done.9.rest_0_
  63.8 1.0 %collective-permute-start.6 = (f32[64,128]{1,0:T(8,128)S(1)}, f32[64,128]{1,0:T(8,128)S(1)}, u32[]{:S(2)}, u32[]{:S(2)}) collective-permute-start(f32[64,128]{1,0:T(8,128)S(1)} %get-tuple-element.38), channel_id=1, source_target_pairs={{0,8},{4,12},{8,0},{12,4},{1,9},{5,13},{9,1},{13,5},{2,10},{6,14},... | collective-permute-start | bytes 98312 | tf_op jit(solution)/shard_map/ppermute | solution.py:329
  64.8 0.0 collective-permute-done.10.rest_1_
  64.8 1.5 %collective-permute-start.7 = (f32[64,128]{1,0:T(8,128)S(1)}, f32[64,128]{1,0:T(8,128)S(1)}, u32[]{:S(2)}, u32[]{:S(2)}) collective-permute-start(f32[64,128]{1,0:T(8,128)S(1)} %get-tuple-element.39), channel_id=1, source_target_pairs={{0,12},{4,8},{8,4},{12,0},{1,13},{5,9},{9,5},{13,1},{2,14},{6,10},... | collective-permute-start | bytes 98312 | tf_op jit(solution)/shard_map/ppermute | solution.py:329
  66.3 0.0 collective-permute-done.12.rest_3_
  66.3 1.6 %part_scores.1.before = f32[2,64,256]{2,1,0:T(8,128)S(1)} custom-call(bf16[2,16384,256]{2,1,0:T(8,128)(2,1)S(1)} %get-tuple-element.40.turned, bf16[64,16,256]{2,1,0:T(8,128)(2,1)S(1)} %collective-permute-done.9.rest_0_, bf16[64,16,256]{2,1,0:T(8,128)(2,1)S(1)} %collective-permute-done.10.rest_1_, bf16[32,16,256]{2,1,0:T(8,128)(2,1)S(1)} %collective-permute-done.11.rest_2_, ...), custom_call_target="tpu_custom_call" | custom-call | tf_op jit(solution)/shard_map/part_scores/pallas_call | solution.py:230
  67.9 0.8 collective-permute-done.14.rest_3_
  68.7 1.8 %late_scores.1 = (f32[64,128]{1,0:T(8,128)S(1)}, f32[64,128]{1,0:T(8,128)S(1)}, f32[64,128]{1,0:T(8,128)S(1)}, f32[64,128]{1,0:T(8,128)S(1)}) custom-call(bf16[2,16384,256]{2,1,0:T(8,128)(2,1)S(1)} %get-tuple-element.40.turned, f32[2,64,256]{2,1,0:T(8,128)S(1)} %part_scores.1.before, s32[1,256]{1,0:T(1,128)S(1)} %select_n.33.own_order, ...), custom_call_target="tpu_custom_call" | custom-call | tf_op jit(solution)/shard_map/late_scores/pallas_call | solution.py:260
  70.5 0.6 collective-permute-start.15
  71.2 2.5 %collective-permute-start.16 = (f32[64,128]{1,0:T(8,128)S(1)}, f32[64,128]{1,0:T(8,128)S(1)}, u32[]{:S(2)}, u32[]{:S(2)}) collective-permute-start(f32[64,128]{1,0:T(8,128)S(1)} %get-tuple-element.49), channel_id=1, source_target_pairs={{0,8},{4,12},{8,0},{12,4},{1,9},{5,13},{9,1},{13,5},{2,10},{6,14},... | collective-permute-start | bytes 98312 | tf_op jit(solution)/shard_map/ppermute | solution.py:329
  73.6 0.0 collective-permute-done.5.refs_1_
  73.6 1.4 %collective-permute-start.17 = (f32[64,128]{1,0:T(8,128)S(1)}, f32[64,128]{1,0:T(8,128)S(1)}, u32[]{:S(2)}, u32[]{:S(2)}) collective-permute-start(f32[64,128]{1,0:T(8,128)S(1)} %get-tuple-element.50), channel_id=1, source_target_pairs={{0,12},{4,8},{8,4},{12,0},{1,13},{5,9},{9,5},{13,1},{2,14},{6,10},... | collective-permute-start | bytes 98312 | tf_op jit(solution)/shard_map/ppermute | solution.py:329
  75.0 0.0 collective-permute-done.6.refs_2_
  75.0 0.0 collective-permute-done.7.refs_3_
  75.0 1.3 %collective-permute-done.16.refs_6_ = f32[64,128]{1,0:T(8,128)S(1)} collective-permute-done((f32[64,128]{1,0:T(8,128)S(1)}, f32[64,128]{1,0:T(8,128)S(1)}, u32[]{:S(2)}, u32[]{:S(2)}) %collective-permute-start.16) | collective-permute-done | bytes 32800 | tf_op jit(solution)/shard_map/ppermute | solution.py:329
  76.3 3.0 %collective-permute-done.17.refs_7_ = f32[64,128]{1,0:T(8,128)S(1)} collective-permute-done((f32[64,128]{1,0:T(8,128)S(1)}, f32[64,128]{1,0:T(8,128)S(1)}, u32[]{:S(2)}, u32[]{:S(2)}) %collective-permute-start.17) | collective-permute-done | bytes 32800 | tf_op jit(solution)/shard_map/ppermute | solution.py:329
  79.3 0.1 reduce.1
  79.4 0.1 collective-permute-start.18
  79.5 1.2 %collective-permute-done.18.other = f32[128,64]{1,0:T(8,128)S(1)} collective-permute-done((f32[128,64]{1,0:T(8,128)S(1)}, f32[128,64]{1,0:T(8,128)S(1)}, u32[]{:S(2)}, u32[]{:S(2)}) %collective-permute-start.18) | collective-permute-done | bytes 32800 | tf_op jit(solution)/shard_map/ppermute | solution.py:329
  80.7 0.7 finish.1
  (6 shorter events, 0.0 us)
Async XLA Ops:
  0.0 16.2 %copy-start = (s32[256]{0:T(256)S(1)}, s32[256]{0:T(256)}, u32[]{:S(2)}) copy-start(s32[256]{0:T(256)} %param.15) | copy-start | bytes 3076
  6.4 43.8 %collective-permute-start = (bf16[256,16384]{1,0:T(8,128)(2,1)}, bf16[256,16384]{1,0:T(8,128)(2,1)}, u32[]{:S(2)}, u32[]{:S(2)}) collective-permute-start(bf16[256,16384]{1,0:T(8,128)(2,1)} %own.1), channel_id=1, source_target_pairs={{0,1},{1,0},{2,3},{3,2},{4,5},{5,4},{6,7},{7,6},{8,9},{9,8},{10,11... | collective-permute-start | bytes 25165832 | tf_op jit(solution)/shard_map/ppermute | solution.py:329
  6.9 22.8 %collective-permute-start.3 = (bf16[64,16,256]{2,1,0:T(8,128)(2,1)S(1)}, bf16[64,16,256]{2,1,0:T(8,128)(2,1)S(1)}, u32[]{:S(2)}, u32[]{:S(2)}) collective-permute-start(bf16[64,16,256]{2,1,0:T(8,128)(2,1)S(1)} %get-tuple-element.29), channel_id=1, source_target_pairs={{0,4},{4,0},{8,12},{12,8},{1,5},{5,1},{9,13},{13,9},{2,6},{6,2},{1... | collective-permute-start | bytes 1572872 | tf_op jit(solution)/shard_map/ppermute | solution.py:329
  9.6 20.2 %collective-permute-start.8 = (bf16[64,16,256]{2,1,0:T(8,128)(2,1)S(1)}, bf16[64,16,256]{2,1,0:T(8,128)(2,1)}, u32[]{:S(2)}, u32[]{:S(2)}) collective-permute-start(bf16[64,16,256]{2,1,0:T(8,128)(2,1)S(1)} %get-tuple-element.29), channel_id=1, source_target_pairs={{0,2},{1,3},{2,0},{3,1},{4,6},{5,7},{6,4},{7,5},{8,10},{9,11},{10,... | collective-permute-start | bytes 1572872 | tf_op jit(solution)/shard_map/ppermute | solution.py:329
  13.1 34.7 %collective-permute-start.2 = (bf16[64,16,256]{2,1,0:T(8,128)(2,1)S(1)}, bf16[64,16,256]{2,1,0:T(8,128)(2,1)S(1)}, u32[]{:S(2)}, u32[]{:S(2)}) collective-permute-start(bf16[64,16,256]{2,1,0:T(8,128)(2,1)S(1)} %get-tuple-element.34.rest_0_), channel_id=1, source_target_pairs={{0,2},{1,3},{2,0},{3,1},{4,6},{5,7},{6,4},{7,5},{8,10},{9,11},{10,... | collective-permute-start | bytes 1572872 | tf_op jit(solution)/shard_map/ppermute | solution.py:329
  13.6 32.6 %collective-permute-start.4 = (bf16[64,16,256]{2,1,0:T(8,128)(2,1)S(1)}, bf16[64,16,256]{2,1,0:T(8,128)(2,1)S(1)}, u32[]{:S(2)}, u32[]{:S(2)}) collective-permute-start(bf16[64,16,256]{2,1,0:T(8,128)(2,1)S(1)} %get-tuple-element.35), channel_id=1, source_target_pairs={{0,8},{4,12},{8,0},{12,4},{1,9},{5,13},{9,1},{13,5},{2,10},{6,14},... | collective-permute-start | bytes 1572872 | tf_op jit(solution)/shard_map/ppermute | solution.py:329
  29.8 2.7 %collective-permute-start.1 = (s32[1,256]{1,0:T(1,128)S(1)}, s32[1,256]{1,0:T(1,128)S(1)}, u32[]{:S(2)}, u32[]{:S(2)}) collective-permute-start(s32[1,256]{1,0:T(1,128)S(1)} %select_n.33.own_order), channel_id=1, source_target_pairs={{0,1},{1,0},{2,3},{3,2},{4,5},{5,4},{6,7},{7,6},{8,9},{9,8},{10,11... | collective-permute-start | bytes 3080 | tf_op jit(solution)/shard_map/ppermute | solution.py:329
  29.8 28.1 %collective-permute-start.11 = (bf16[32,16,256]{2,1,0:T(8,128)(2,1)S(1)}, bf16[32,16,256]{2,1,0:T(8,128)(2,1)S(1)}, u32[]{:S(2)}, u32[]{:S(2)}) collective-permute-start(bf16[32,16,256]{2,1,0:T(8,128)(2,1)S(1)} %get-tuple-element.43), channel_id=1, source_target_pairs={{0,12},{4,8},{8,4},{12,0},{1,13},{5,9},{9,5},{13,1},{2,14},{6,10},... | collective-permute-start | bytes 786440 | tf_op jit(solution)/shard_map/ppermute | solution.py:329
  32.5 31.3 %collective-permute-start.9 = (bf16[64,16,256]{2,1,0:T(8,128)(2,1)}, bf16[64,16,256]{2,1,0:T(8,128)(2,1)S(1)}, u32[]{:S(2)}, u32[]{:S(2)}) collective-permute-start(bf16[64,16,256]{2,1,0:T(8,128)(2,1)} %collective-permute-done.8), channel_id=1, source_target_pairs={{0,4},{4,0},{8,12},{12,8},{1,5},{5,1},{9,13},{13,9},{2,6},{6,2},{1... | collective-permute-start | bytes 1572872 | tf_op jit(solution)/shard_map/ppermute | solution.py:329
  46.2 18.6 %collective-permute-start.10 = (bf16[64,16,256]{2,1,0:T(8,128)(2,1)S(1)}, bf16[64,16,256]{2,1,0:T(8,128)(2,1)S(1)}, u32[]{:S(2)}, u32[]{:S(2)}) collective-permute-start(bf16[64,16,256]{2,1,0:T(8,128)(2,1)S(1)} %collective-permute-done.4.rest_3_), channel_id=1, source_target_pairs={{0,2},{1,3},{2,0},{3,1},{4,6},{5,7},{6,4},{7,5},{8,10},{9,11},{10,... | collective-permute-start | bytes 1572872 | tf_op jit(solution)/shard_map/ppermute | solution.py:329
  47.7 10.8 %collective-permute-start.13 = (bf16[32,16,256]{2,1,0:T(8,128)(2,1)}, bf16[32,16,256]{2,1,0:T(8,128)(2,1)S(1)}, u32[]{:S(2)}, u32[]{:S(2)}) collective-permute-start(bf16[32,16,256]{2,1,0:T(8,128)(2,1)} %get-tuple-element.46), channel_id=1, source_target_pairs={{0,12},{4,8},{8,4},{12,0},{1,13},{5,9},{9,5},{13,1},{2,14},{6,10},... | collective-permute-start | bytes 786440 | tf_op jit(solution)/shard_map/ppermute | solution.py:329
  57.9 8.4 %collective-permute-start.12 = (bf16[32,16,256]{2,1,0:T(8,128)(2,1)S(1)}, bf16[32,16,256]{2,1,0:T(8,128)(2,1)S(1)}, u32[]{:S(2)}, u32[]{:S(2)}) collective-permute-start(bf16[32,16,256]{2,1,0:T(8,128)(2,1)S(1)} %collective-permute-done.11.rest_2_), channel_id=1, source_target_pairs={{0,2},{1,3},{2,0},{3,1},{4,6},{5,7},{6,4},{7,5},{8,10},{9,11},{10,... | collective-permute-start | bytes 786440 | tf_op jit(solution)/shard_map/ppermute | solution.py:329
  58.5 10.2 %collective-permute-start.14 = (bf16[32,16,256]{2,1,0:T(8,128)(2,1)S(1)}, bf16[32,16,256]{2,1,0:T(8,128)(2,1)S(1)}, u32[]{:S(2)}, u32[]{:S(2)}) collective-permute-start(bf16[32,16,256]{2,1,0:T(8,128)(2,1)S(1)} %collective-permute-done.13.rest_2_), channel_id=1, source_target_pairs={{0,2},{1,3},{2,0},{3,1},{4,6},{5,7},{6,4},{7,5},{8,10},{9,11},{10,... | collective-permute-start | bytes 786440 | tf_op jit(solution)/shard_map/ppermute | solution.py:329
  60.0 13.6 %collective-permute-start.5 = (f32[64,128]{1,0:T(8,128)S(1)}, f32[64,128]{1,0:T(8,128)S(1)}, u32[]{:S(2)}, u32[]{:S(2)}) collective-permute-start(f32[64,128]{1,0:T(8,128)S(1)} %get-tuple-element.37), channel_id=1, source_target_pairs={{0,4},{4,0},{8,12},{12,8},{1,5},{5,1},{9,13},{13,9},{2,6},{6,2},{1... | collective-permute-start | bytes 98312 | tf_op jit(solution)/shard_map/ppermute | solution.py:329
  63.8 11.2 %collective-permute-start.6 = (f32[64,128]{1,0:T(8,128)S(1)}, f32[64,128]{1,0:T(8,128)S(1)}, u32[]{:S(2)}, u32[]{:S(2)}) collective-permute-start(f32[64,128]{1,0:T(8,128)S(1)} %get-tuple-element.38), channel_id=1, source_target_pairs={{0,8},{4,12},{8,0},{12,4},{1,9},{5,13},{9,1},{13,5},{2,10},{6,14},... | collective-permute-start | bytes 98312 | tf_op jit(solution)/shard_map/ppermute | solution.py:329
  64.8 10.2 %collective-permute-start.7 = (f32[64,128]{1,0:T(8,128)S(1)}, f32[64,128]{1,0:T(8,128)S(1)}, u32[]{:S(2)}, u32[]{:S(2)}) collective-permute-start(f32[64,128]{1,0:T(8,128)S(1)} %get-tuple-element.39), channel_id=1, source_target_pairs={{0,12},{4,8},{8,4},{12,0},{1,13},{5,9},{9,5},{13,1},{2,14},{6,10},... | collective-permute-start | bytes 98312 | tf_op jit(solution)/shard_map/ppermute | solution.py:329
  70.5 4.5 %collective-permute-start.15 = (f32[64,128]{1,0:T(8,128)S(1)}, f32[64,128]{1,0:T(8,128)S(1)}, u32[]{:S(2)}, u32[]{:S(2)}) collective-permute-start(f32[64,128]{1,0:T(8,128)S(1)} %get-tuple-element.48), channel_id=1, source_target_pairs={{0,4},{4,0},{8,12},{12,8},{1,5},{5,1},{9,13},{13,9},{2,6},{6,2},{1... | collective-permute-start | bytes 98312 | tf_op jit(solution)/shard_map/ppermute | solution.py:329
  71.2 5.2 %collective-permute-start.16 = (f32[64,128]{1,0:T(8,128)S(1)}, f32[64,128]{1,0:T(8,128)S(1)}, u32[]{:S(2)}, u32[]{:S(2)}) collective-permute-start(f32[64,128]{1,0:T(8,128)S(1)} %get-tuple-element.49), channel_id=1, source_target_pairs={{0,8},{4,12},{8,0},{12,4},{1,9},{5,13},{9,1},{13,5},{2,10},{6,14},... | collective-permute-start | bytes 98312 | tf_op jit(solution)/shard_map/ppermute | solution.py:329
  73.6 5.7 %collective-permute-start.17 = (f32[64,128]{1,0:T(8,128)S(1)}, f32[64,128]{1,0:T(8,128)S(1)}, u32[]{:S(2)}, u32[]{:S(2)}) collective-permute-start(f32[64,128]{1,0:T(8,128)S(1)} %get-tuple-element.50), channel_id=1, source_target_pairs={{0,12},{4,8},{8,4},{12,0},{1,13},{5,9},{9,5},{13,1},{2,14},{6,10},... | collective-permute-start | bytes 98312 | tf_op jit(solution)/shard_map/ppermute | solution.py:329
  79.4 1.3 %collective-permute-start.18 = (f32[128,64]{1,0:T(8,128)S(1)}, f32[128,64]{1,0:T(8,128)S(1)}, u32[]{:S(2)}, u32[]{:S(2)}) collective-permute-start(f32[128,64]{1,0:T(8,128)S(1)} %get-tuple-element.52), channel_id=1, source_target_pairs={{0,1},{1,0},{2,3},{3,2},{4,5},{5,4},{6,7},{7,6},{8,9},{9,8},{10,11... | collective-permute-start | bytes 98312 | tf_op jit(solution)/shard_map/ppermute | solution.py:329
